TPU v7x, 128 devices: a whole 4x4x4 slice. The times are simulated.
128 devices in a mesh: tm: 16 (over z, x), rows: 8 (over y, core).
Axes of the slice: x: 4, y: 4, z: 4, core: 2. Of those that a mesh axis runs over, the one named last changes fastest.
Arguments:
- features: float32 [1048576, 512], P(('tm', 'rows'))
- response_lines: float32 [1048576, 128], P(('tm', 'rows'))
- row_counts: int32 [16], replicated, may hold values from 32768 to 65536, as said below
- ridge_codes: int32 [16], replicated, may hold values from 2 to 33
Outputs:
- forecast: bfloat16 [1048576, 128], P(('tm', 'rows'))
- partition_mse: float32 [16], P('tm')
Inputs may be any that keep to these rules, and one draw needn't show every extreme that they name: `row_counts`: each count is a multiple of 128, at least half of 65536 and at most 65536.
All inputs are finite; a program needn't handle non-finite values.
Results may differ from a plain program's by a relative error of at most 0.001.
Values sent between devices are 32-bit elements; how exact they have to be, the bound alone decides.
A program may use at most 128 MiB of HBM per device.

v0:
```python
import jax
import jax.numpy as jnp
from jax import lax
from jax.sharding import Mesh
from jax.sharding import PartitionSpec as P

TM = ("tm_0", "tm_1")
TM_ROWS = ("tm_0", "tm_1", "rows")


def neutral_like(value, identity):
    return jax.tree.map(
        lambda a, e: jnp.broadcast_to(jnp.asarray(e, a.dtype), a.shape), value, identity
    )


def prefix_by_axis(value, axes, combine, identity):
    before = start = neutral_like(value, identity)
    so_far = value
    for axis in reversed(axes):
        count, here = (lax.axis_size(axis), lax.axis_index(axis))
        pieces = jax.tree.map(lambda part: lax.all_gather(part, axis), so_far)
        inside, so_far = (start, start)
        for k in range(count):
            passed = k < here
            so_far = combine(so_far, jax.tree.map(lambda part: part[k], pieces))
            inside = jax.tree.map(lambda new, old: jnp.where(passed, new, old), so_far, inside)
        before = combine(inside, before)
    return before


def in_blocks(value, dim, count):
    shape = value.shape
    pieces = value.reshape(*shape[:dim], count, shape[dim] // count, *shape[dim + 1 :])
    return jnp.moveaxis(pieces, dim, 0)


def summed_on_arrival(value, axis, dim):
    count = lax.axis_size(axis)
    pieces = lax.all_to_all(in_blocks(value, dim, count), axis, 0, 0, tiled=True)
    return jnp.sum(pieces, axis=0)


def sent_together(arrays, axis, dim, along):
    both = jnp.concatenate(arrays, axis=along)
    out, at, finished = (summed_on_arrival(both, axis, dim), 0, [])
    for a in arrays:
        finished.append(lax.slice_in_dim(out, at, at + a.shape[along], axis=along))
        at += a.shape[along]
    return tuple(finished)


def turned_gather(arrays, axis, dims):
    turned = [jnp.moveaxis(a, dim, 0) for a, dim in zip(arrays, dims)]
    widths = [t[0].size for t in turned]
    both = jnp.concatenate([t.reshape(-1, w) for t, w in zip(turned, widths)], axis=1)
    out = lax.all_gather(both, axis, axis=0, tiled=True)
    pieces = jnp.split(out, [sum(widths[:k]) for k in range(1, len(widths))], axis=1)
    return tuple(
        (
            jnp.moveaxis(b.reshape(-1, *t.shape[1:]), 0, dim)
            for b, t, dim in zip(pieces, turned, dims)
        )
    )


def from_everyone(value, axis):
    count = lax.axis_size(axis)
    return lax.all_to_all(
        jnp.broadcast_to(value[None], (count, *value.shape)), axis, 0, 0, tiled=True
    )


def of_everyone(value, axis):
    return from_everyone(value, axis).sum(axis=0)


def add_pair(earlier, later):
    return (earlier[0] + later[0], earlier[1] + later[1])


def time_prefix(gram_fragment, cross_piece):
    zeros_pair = (jnp.zeros_like(gram_fragment), jnp.zeros_like(cross_piece))
    return prefix_by_axis((gram_fragment, cross_piece), TM, add_pair, zeros_pair)


def ridge_solve(gram_sum, cross_sum, ridge_value):
    identity = jnp.eye(gram_sum.shape[0], dtype=jnp.float32)
    lower_factor = jnp.linalg.cholesky(gram_sum + ridge_value * identity)
    return jax.scipy.linalg.cho_solve((lower_factor, True), cross_sum)


def body(features, response_lines, row_counts, ridge_codes):
    rows_dev = features.shape[0]
    width_targets = response_lines.shape[1]
    time_index = lax.axis_index(TM)
    row_index = lax.axis_index("rows")
    positions = row_index * rows_dev + lax.iota(jnp.int32, rows_dev)
    usable_line_flags = (positions < row_counts[time_index]).astype(jnp.float32)
    weighted = features * usable_line_flags[:, None]
    contract_product = (((0,), (0,)), ((), ()))
    gram_part = lax.dot_general(
        weighted,
        features,
        contract_product,
        precision=lax.Precision.HIGHEST,
        preferred_element_type=jnp.float32,
    )
    cross_part = lax.dot_general(
        weighted,
        response_lines,
        contract_product,
        precision=lax.Precision.HIGHEST,
        preferred_element_type=jnp.float32,
    )
    gram_share, cross_share = sent_together((gram_part, cross_part), "rows", 0, 1)
    before_gram, before_cross = time_prefix(gram_share, cross_share)
    gram_fragment, cross_piece = (before_gram, before_cross)
    gram_used, cross_used = turned_gather((gram_fragment, cross_piece), "rows", (0, 0))
    counts_float = row_counts.astype(jnp.float32)
    seen_through = jnp.cumsum(counts_float)[time_index]
    earlier_index = jnp.maximum(time_index - 1, 0)
    seen_before = seen_through - counts_float[time_index]
    is_first = (time_index == 0).astype(jnp.float32)
    ridge_value = ridge_codes[earlier_index].astype(jnp.float32) * seen_before / 16.0 + is_first
    solved = ridge_solve(gram_used, cross_used, ridge_value)
    weights_prev = solved * (1.0 - is_first)
    predicted_result = (
        jnp.dot(
            features,
            weights_prev,
            precision=lax.Precision.HIGHEST,
            preferred_element_type=jnp.float32,
        )
        * usable_line_flags[:, None]
    )
    residual_here = jnp.sum(usable_line_flags[:, None] * (response_lines - predicted_result) ** 2)
    error_total = of_everyone(residual_here, "rows")
    partition_mse = error_total / (counts_float[time_index] * width_targets)
    return (predicted_result.astype(jnp.bfloat16), partition_mse.reshape(1))


def solution(mesh):
    finer = Mesh(mesh.devices.reshape(4, 4, mesh.shape["rows"]), ("tm_0", "tm_1", "rows"))
    placed = (P(TM_ROWS, None), P(TM_ROWS, None), P(), P())
    return jax.shard_map(
        body, mesh=finer, in_specs=placed, out_specs=(P(TM_ROWS, None), P(TM)), check_vma=False
    )
```

profile of v0, /device:TPU:65, one launch (start us, length us, event | category | flops | bytes accessed | tf_op | source)
XLA Modules:
  0.0 338.0 jit_solution(11522218888690972044)
XLA Ops:
  7.2 1.2 dynamic_slice.13
  9.1 35.5 %fusion.2 = f32[512,512]{0,1:T(8,128)S(1)} fusion(f32[8192,512]{1,0:T(8,128)} %param.4, f32[8192]{0:T(1024)S(1)} %fusion.65), kind=kOutput, calls=%fused_computation.4 | convolution fusion | flops 25773998080 | bytes 17858560 | tf_op jit(solution)/shard_map/dot_general | solution.py:102
  44.6 13.4 %fusion = f32[512,128]{0,1:T(8,128)S(1)} fusion(f32[8192,128]{1,0:T(8,128)} %param.5, f32[8192,512]{1,0:T(8,128)S(1)} %copy-done, f32[8192]{0:T(1024)S(1)} %fusion.65), kind=kOutput, calls=%fused_computation.2 | convolution fusion | flops 6446645248 | bytes 21266432 | tf_op jit(solution)/shard_map/dot_general | solution.py:109
  58.1 1.5 copy.59
  59.5 5.1 %all-to-all-start = ((f32[8,64,640]{2,1,0:T(8,128)}), f32[8,64,640]{2,1,0:T(8,128)S(1)}, u32[]{:S(2)}, u32[]{:S(2)}) async-start(f32[8,64,640]{2,1,0:T(8,128)} %bitcast.1), calls=%async_computation | async-start | bytes 2621440 | tf_op jit(solution)/shard_map/all_to_all | solution.py:40
  64.7 17.9 %all-to-all-done = f32[8,64,640]{2,1,0:T(8,128)S(1)} async-done(((f32[8,64,640]{2,1,0:T(8,128)}), f32[8,64,640]{2,1,0:T(8,128)S(1)}, u32[]{:S(2)}, u32[]{:S(2)}) %all-to-all-start) | async-done | bytes 1310752 | tf_op jit(solution)/shard_map/all_to_all | solution.py:40
  82.7 9.7 %all-gather.1 = f32[256,128]{1,0:T(8,128)S(1)} all-gather(f32[64,128]{1,0:T(8,128)S(1)} %slice.251), channel_id=3, replica_groups=mesh['tm_0'=4,'tm_1'=4,'rows'=8] {'tm_1'}, dimensions={0}, use_global_device_ids=true | all-gather | bytes 163840 | tf_op jit(solution)/shard_map/all_gather | solution.py:22
  92.4 7.9 %all_gather.28 = f32[4,64,128]{2,1,0:T(8,128)S(1)} all-gather(f32[1,64,128]{2,1,0:T(8,128)S(1)} %fusion.64), channel_id=1, replica_groups=mesh['tm_0'=4,'tm_1'=4,'rows'=8] {'tm_0'}, dimensions={0}, use_global_device_ids=true | all-gather | bytes 163840 | tf_op jit(solution)/shard_map/all_gather | solution.py:22
  100.3 9.9 %all-gather = f32[256,512]{1,0:T(8,128)S(1)} all-gather(f32[64,512]{1,0:T(8,128)S(1)} %slice.242), channel_id=2, replica_groups=mesh['tm_0'=4,'tm_1'=4,'rows'=8] {'tm_1'}, dimensions={0}, use_global_device_ids=true | all-gather | bytes 655360 | tf_op jit(solution)/shard_map/all_gather | solution.py:22
  110.2 10.2 %all_gather.25 = f32[4,64,512]{2,1,0:T(8,128)S(1)} all-gather(f32[1,64,512]{2,1,0:T(8,128)S(1)} %fusion.37), channel_id=1, replica_groups=mesh['tm_0'=4,'tm_1'=4,'rows'=8] {'tm_0'}, dimensions={0}, use_global_device_ids=true | all-gather | bytes 655360 | tf_op jit(solution)/shard_map/all_gather | solution.py:22
  121.3 6.0 %copy.71 = f32[8192,128]{0,1:T(8,128)} copy(f32[8192,128]{1,0:T(8,128)} %param.5) | data formatting | bytes 8388608 | tf_op args[1]
  131.9 25.4 %all-gather.4.cloned.1.call-done = f32[512,640]{1,0:T(8,128)} async-done(((f32[64,640]{1,0:T(8,128)}), f32[512,640]{1,0:T(8,128)}) %all-gather.4.cloned.1.call-update) | async-done | bytes 1310736 | tf_op jit(solution)/shard_map/all_gather | solution.py:57
  157.4 1.3 split.5
  159.7 11.7 %cholesky.103 = f32[128,128]{1,0:T(8,128)S(1)} custom-call(f32[128,128]{1,0:T(8,128)S(1)} %cholesky.263), custom_call_target="Cholesky" | custom-call | tf_op jit(solution)/shard_map/jit(cholesky)/cholesky | solution.py:89
  171.6 9.8 %custom-call.34 = f32[1,128,128]{1,2,0:T(8,128)S(1)} custom-call(f32[1,128,128]{2,1,0:T(8,128)S(1)} %get-tuple-element.57), custom_call_target="InvertDiagBlocksLowerTriangular" | custom-call | tf_op jit(solution)/shard_map/jit(cholesky)/cholesky | solution.py:89
  182.2 11.7 %cholesky.215 = f32[128,128]{1,0:T(8,128)S(1)} custom-call(f32[128,128]{1,0:T(8,128)S(1)} %cholesky.267), custom_call_target="Cholesky" | custom-call | tf_op jit(solution)/shard_map/jit(cholesky)/cholesky | solution.py:89
  194.0 10.0 %custom-call.35 = f32[1,128,128]{1,2,0:T(8,128)S(1)} custom-call(f32[1,128,128]{2,1,0:T(8,128)S(1)} %get-tuple-element.55), custom_call_target="InvertDiagBlocksLowerTriangular" | custom-call | tf_op jit(solution)/shard_map/jit(cholesky)/cholesky | solution.py:89
  205.1 11.7 %cholesky.236 = f32[128,128]{1,0:T(8,128)S(1)} custom-call(f32[128,128]{1,0:T(8,128)S(1)} %cholesky.272), custom_call_target="Cholesky" | custom-call | tf_op jit(solution)/shard_map/jit(cholesky)/cholesky | solution.py:89
  217.0 9.8 %custom-call.36 = f32[1,128,128]{1,2,0:T(8,128)S(1)} custom-call(f32[1,128,128]{2,1,0:T(8,128)S(1)} %get-tuple-element.53), custom_call_target="InvertDiagBlocksLowerTriangular" | custom-call | tf_op jit(solution)/shard_map/jit(cholesky)/cholesky | solution.py:89
  227.6 11.9 %cholesky.253 = f32[128,128]{1,0:T(8,128)S(1)} custom-call(f32[128,128]{1,0:T(8,128)S(1)} %convolution_subtract_fusion.8), custom_call_target="Cholesky" | custom-call | tf_op jit(solution)/shard_map/jit(cholesky)/cholesky | solution.py:89
  244.2 8.1 %while.1 = (s32[]{:T(128)}, f32[512,512]{0,1:T(8,128)S(1)}, s32[4,2]{0,1:T(2,128)S(1)}, f32[4,128,128]{2,1,0:T(8,128)S(1)}, s32[]{:T(128)}) while((s32[]{:T(128)}, f32[512,512]{0,1:T(8,128)S(1)}, s32[4,2]{0,1:T(2,128)S(1)}, f32[4,128,128]{2,1,0:T(8,128)S(1)}, s32[]{:T(128)}) %tuple.41), condition=%wide.while_cond, body=%wide.while_body.sunk | while | flops 2 | bytes 393329 | solution.py:90
  244.8 1.3 dynamic-slice.8
  246.8 1.3 dynamic-slice.8
  248.9 1.3 dynamic-slice.8
  250.9 1.3 dynamic-slice.8
  252.3 39.3 %custom-call.37 = f32[4,128,128]{1,2,0:T(8,128)S(1)} custom-call(f32[4,128,128]{2,1,0:T(8,128)S(1)} %get-tuple-element.9), custom_call_target="InvertDiagBlocksLowerTriangular" | custom-call | tf_op jit(solution)/shard_map/jit(_cho_solve)/triangular_solve | solution.py:90
  292.7 1.1 convolution_subtract_fusion.5
  294.2 1.2 convolution_subtract_fusion.4
  295.7 1.3 convolution_subtract_fusion.7
  299.0 18.9 %multiply_reduce_fusion = (f32[]{:T(128)}, bf16[8192,128]{0,1:T(8,128)(2,1)S(1)}) fusion(f32[8192,128]{0,1:T(8,128)} %copy.71, f32[8192]{0:T(1024)S(1)} %fusion.65, f32[8192,512]{1,0:T(8,128)} %param.4, f32[128,128]{1,0:T(8,128)S(1)} %fusion.59, f32[128,128]{1,0:T(8,128)S(1)} %fusion.57, f32[128,128]{1,0:T(8,128)S(1)} %fusion.55, ...), kind=kOutput, calls=%fused_computation.10 | convolution fusion | flops 6449004544 | bytes 23363592 | tf_op jit(solution)/shard_map/dot_general | solution.py:129
  317.9 2.4 copy.73
  321.0 7.5 %all_to_all.11 = f32[8,1,1]{2,1,0:T(1,128)S(1)} all-to-all(f32[8,1,1]{2,1,0:T(1,128)S(1)} %broadcast_in_dim.10), channel_id=1, replica_groups=mesh['tm_0'=4,'tm_1'=4,'rows'=8] {'rows'}, dimensions={0} | all-to-all | bytes 64 | tf_op jit(solution)/shard_map/all_to_all | solution.py:69
  (87 shorter events, 17.5 us)
Async XLA Ops:
  9.1 35.5 %copy-start = (f32[8192,512]{1,0:T(8,128)S(1)}, f32[8192,512]{1,0:T(8,128)}, u32[]{:S(2)}) copy-start(f32[8192,512]{1,0:T(8,128)} %param.4) | copy-start | bytes 50331652
  59.5 23.1 %all-to-all-start = ((f32[8,64,640]{2,1,0:T(8,128)}), f32[8,64,640]{2,1,0:T(8,128)S(1)}, u32[]{:S(2)}, u32[]{:S(2)}) async-start(f32[8,64,640]{2,1,0:T(8,128)} %bitcast.1), calls=%async_computation | async-start | bytes 2621440 | tf_op jit(solution)/shard_map/all_to_all | solution.py:40
  64.7 92.7 %all-gather.4.cloned.1.call-start = ((), (), s32[]{:S(2)}) async-start(), calls=%async_computation.2 | async-start | bytes 1474560 | tf_op jit(solution)/shard_map/all_gather | solution.py:57
  121.3 6.1 %copy-start.1 = (s32[16]{0:T(128)S(1)}, s32[16]{0:T(128)}, u32[]{:S(2)}) copy-start(s32[16]{0:T(128)} %param.7) | copy-start | bytes 196
  121.3 7.4 %copy-start.2 = (s32[16]{0:T(128)S(1)}, s32[16]{0:T(128)}, u32[]{:S(2)}) copy-start(s32[16]{0:T(128)} %param.6) | copy-start | bytes 196
Sparse Core Ops, SparseCore 0:
  121.4 35.9 all-gather.3
where the time goes:
time: 344 us; the launch traced here: 338 us
  other arithmetic  121 us (35%)
  matrix products  77.4 us (23%)
  blocking collectives  45.2 us (13%)
  waiting for transfers between devices  43.4 us (13%)
  local copies, waits for them, and re-layouts  24.3 us (7%)
  between operations  21.7 us (6%)
  starting transfers between devices  5.15 us (1%)
    another operation x14, other arithmetic, ridge_solve(): lower_factor = jnp.linalg.cholesky(gram_sum + ridge_value * identity)  78.7 us
    another operation x3, other arithmetic, ridge_solve(): return jax.scipy.linalg.cho_solve((lower_factor, True), cross_sum)  39.4 us
    all_gather x4, blocking collectives, prefix_by_axis(): pieces = jax.tree.map(lambda part: lax.all_gather(part, axis), so_far)  37.6 us
    dot_general x1, matrix products, body(): lax.dot_general(weighted, features, contract_product, precision=lax.Preci...  35.5 us
    all_gather x1, waiting for transfers between devices, turned_gather(): out = lax.all_gather(both, axis, axis=0, tiled=True)  25.4 us
    dot_general x1, matrix products, body(): jnp.dot(features, weights_prev, precision=lax.Precision.HIGHEST, preferre...  18.9 us
    all_to_all x1, waiting for transfers between devices, summed_on_arrival(): lax.all_to_all(in_blocks(value, dim, count), axis, 0, 0, tiled=True)  17.9 us
    dot_general x1, matrix products, body(): lax.dot_general(weighted, response_lines, contract_product, precision=lax...  13.4 us
  transfers between devices with their start and end apart: 2, of which 2 were waited for; matrix products, arithmetic and copies ran while one was open for 2% of the time, Pallas kernels for 0%

commit v1 on v0

v1 whole, which is shorter than its diff:
```python
import functools

import jax
import jax.numpy as jnp
from jax import lax
from jax.experimental import pallas as pl
from jax.experimental.pallas import tpu as pltpu
from jax.sharding import Mesh
from jax.sharding import PartitionSpec as P

TM = ("tm_0", "tm_1")
TM_ROWS = ("tm_0", "tm_1", "rows")
F32 = jnp.float32
BF = jnp.bfloat16
B = 128
WIDE = 16
MESH = pl.DeviceIdType.MESH


def halves_of(x):
    high = x.astype(BF)
    return high, (x - high.astype(F32)).astype(BF)


def thirds_of(x):
    high = x.astype(BF)
    left = x - high.astype(F32)
    middle = left.astype(BF)
    return high, middle, (left - middle.astype(F32)).astype(BF)


def mxu(left, right, dims=(1, 0)):
    contract = (((dims[0],), (dims[1],)), ((), ()))
    return lax.dot_general(left, right, contract, preferred_element_type=F32)


def full_dot(a, b, dims=(1, 0)):
    ah, am, al = thirds_of(a)
    bh, bm, bl = thirds_of(b)
    left = jnp.concatenate([ah, ah, am, am, ah, al], axis=dims[0])
    right = jnp.concatenate([bh, bm, bh, bm, bl, bh], axis=dims[1])
    return mxu(left, right, dims)


def gram_kernel(tile, valid_ref, x_ref, y_ref, out_ref, upper, lower, turned):
    step = pl.program_id(0)
    f, r = x_ref.shape[1], y_ref.shape[1]
    half = f // 2

    @pl.when(step == 0)
    def _():
        for acc in (upper, lower, turned):
            acc[...] = jnp.zeros_like(acc)

    rows = step * tile + lax.broadcasted_iota(jnp.int32, (tile, 1), 0)
    valid = rows < valid_ref[0]
    xh, xl = halves_of(jnp.where(valid, x_ref[...], 0.0))
    yh, yl = halves_of(y_ref[...])
    upper[...] += mxu(xh[:, :half], jnp.concatenate([yh, yl, xl, xh], axis=1), (0, 0))
    lower[...] += mxu(xh[:, half:], jnp.concatenate([yh, yl, xl, xh[:, half:]], axis=1), (0, 0))
    turned[...] += mxu(yh, xl, (0, 0))

    @pl.when(step == pl.num_programs(0) - 1)
    def _():
        def strip(i):
            acc = upper if i * B < half else lower
            return acc, pl.ds(i * B % half, B), 0 if i * B < half else half

        for i in range(f // B):
            a = pl.ds(i * B, B)
            acc, here, skipped = strip(i)
            for j in range(i, f // B):
                mirror, there, _ = strip(j)
                b = pl.ds(j * B, B)
                out_ref[a, b] = acc[here, pl.ds(2 * r + f + j * B - skipped, B)]
                out_ref[a, b] += acc[here, pl.ds(2 * r + j * B, B)]
                out_ref[a, b] += mirror[there, pl.ds(2 * r + i * B, B)].T
            out_ref[a, pl.ds(f, r)] = acc[here, pl.ds(0, r)] + acc[here, pl.ds(r, r)] + turned[:, a].T


def gram_and_cross(features, targets, valid):
    n, f = features.shape
    r = targets.shape[1]
    tile = 1024
    return pl.pallas_call(
        functools.partial(gram_kernel, tile),
        grid=(n // tile,),
        in_specs=[
            pl.BlockSpec(memory_space=pltpu.SMEM),
            pl.BlockSpec((tile, f), lambda i: (i, 0)),
            pl.BlockSpec((tile, r), lambda i: (i, 0)),
        ],
        out_specs=pl.BlockSpec((f, f + r), lambda i: (0, 0)),
        out_shape=jax.ShapeDtypeStruct((f, f + r), F32),
        scratch_shapes=[
            pltpu.VMEM((f // 2, 2 * f + 2 * r), F32),
            pltpu.VMEM((f // 2, 3 * f // 2 + 2 * r), F32),
            pltpu.VMEM((r, f), F32),
        ],
        compiler_params=pltpu.CompilerParams(vmem_limit_bytes=40 * 2**20),
        name="gram",
    )(valid, features, targets)


def row_of(x, s):
    return jnp.take_along_axis(x, jnp.full((8, B), s, jnp.int32), axis=0)


def column_of(x, c):
    return jnp.broadcast_to(x[:, c : c + 1], (8, B))


def negative_inverse(block):
    block = list(block)
    sub = lax.broadcasted_iota(jnp.int32, (8, B), 0)
    lane = lax.broadcasted_iota(jnp.int32, (8, B), 1)
    halves = WIDE // 8
    steps = B // WIDE
    for g in range(steps):
        mine = [halves * g + h for h in range(halves)]
        ahead = [halves * (g + 1) + h for h in range(halves)] if g + 1 < steps else []
        lo = WIDE * g
        inside = (lane >= lo) & (lane < lo + WIDE)
        cols = [[column_of(block[m], lo + c) for m in mine] for c in range(WIDE)]
        rows = jnp.concatenate([block[m] for m in mine], axis=0)
        right = [
            jnp.where(inside, jnp.where(lane - lo - 8 * h == sub, -1.0, 0.0), block[m])
            for h, m in enumerate(mine)
        ]
        later = {j: [column_of(block[j], lo + c) for c in range(WIDE)] for j in ahead}
        for p in range(WIDE // 2):
            r0, r1 = 2 * p, 2 * p + 1
            h, s0, s1 = r0 // 8, r0 % 8, r0 % 8 + 1
            a, b, c = row_of(cols[r0][h], s0), row_of(cols[r1][h], s0), row_of(cols[r1][h], s1)
            inverse = pl.reciprocal(a * c - b * b)
            at0, at1 = sub == s0, sub == s1
            both = at0 | at1
            n0, n1 = [], []
            for k in range(halves):
                x0 = cols[r0][k] * c - cols[r1][k] * b
                x1 = cols[r1][k] * a - cols[r0][k] * b
                if k == h:
                    x0 = jnp.where(at0, -c, jnp.where(at1, b, x0))
                    x1 = jnp.where(at0, b, jnp.where(at1, -a, x1))
                n0.append(x0)
                n1.append(x1)

            def swept(column):
                u, v = row_of(column[h], s0), row_of(column[h], s1)
                out = []
                for k in range(halves):
                    old = jnp.where(both, 0.0, column[k]) if k == h else column[k]
                    out.append(old - (n0[k] * u + n1[k] * v) * inverse)
                return out

            for q in range(r1 + 1, WIDE):
                cols[q] = swept(cols[q])
            right = swept(right)
        outer = full_dot(rows, jnp.concatenate(right, axis=0), (0, 0))
        terms = [row_of(right[c // 8], c % 8) for c in range(WIDE)] if ahead else None
        for j in range(B // 8):
            if j in mine:
                block[j] = right[j - mine[0]]
            elif j in ahead:
                value = jnp.where(inside, 0.0, block[j])
                for c in range(WIDE):
                    value = value - later[j][c] * terms[c]
                block[j] = value
            else:
                block[j] = jnp.where(inside, 0.0, block[j]) - outer[8 * j : 8 * j + 8, :]
    return jnp.concatenate(block, axis=0)


def solve_in_place(system, ridge):
    f, width = system.shape
    count = f // B
    diagonal = lax.broadcasted_iota(jnp.int32, (B, B), 0) == lax.broadcasted_iota(jnp.int32, (B, B), 1)
    for j in range(count):
        here = pl.ds(j * B, B)
        block = system[here, here] + jnp.where(diagonal, ridge, 0.0)
        inverse = negative_inverse([block[8 * i : 8 * i + 8, :] for i in range(B // 8)])
        rest = system[here, pl.ds((j + 1) * B, width - (j + 1) * B)]
        turned = full_dot(inverse, rest)
        system[here, pl.ds((j + 1) * B, width - (j + 1) * B)] = turned
        for k in range(j + 1, count):
            at = (k - j - 1) * B
            part = pl.ds(k * B, width - k * B)
            system[pl.ds(k * B, B), part] += full_dot(rest[:, at : at + B], turned[:, at:], (0, 0))
    last = pl.ds(f, width - f)
    for j in range(count - 2, -1, -1):
        here = pl.ds(j * B, B)
        behind = pl.ds((j + 1) * B, f - (j + 1) * B)
        system[here, last] += full_dot(system[here, behind], system[behind, last])


def fit_kernel(tile, valid_ref, ridge_ref, system_ref, x_hbm, y_hbm, out_ref, error_ref, system, x, y, sems):
    n, f = x.shape
    r = y.shape[1]
    get_x = pltpu.make_async_copy(x_hbm, x, sems.at[0])
    get_y = pltpu.make_async_copy(y_hbm, y, sems.at[1])
    get_x.start()
    get_y.start()
    for j in range(f // B):
        upper = (pl.ds(j * B, B), pl.ds(j * B, f + r - j * B))
        system[upper] = system_ref[upper]
    solve_in_place(system, ridge_ref[0])
    weights = -system[:, pl.ds(f, r)] * ridge_ref[1]
    wh, wl = halves_of(weights)
    both = jnp.concatenate([wh, wl], axis=1)
    get_x.wait()
    get_y.wait()
    error_ref[...] = jnp.zeros_like(error_ref)

    @pl.loop(0, n // tile)
    def _(i):
        here = pl.ds(pl.multiple_of(i * tile, tile), tile)
        xh, xl = halves_of(x[here, :])
        first = mxu(xh, both)
        value = first[:, :r] + first[:, r:] + mxu(xl, wh)
        valid = i * tile + lax.broadcasted_iota(jnp.int32, (tile, r), 0) < valid_ref[0]
        value = jnp.where(valid, value, 0.0)
        out_ref[here, :] = value.astype(BF)
        gap = jnp.where(valid, y[here, :] - value, 0.0)
        error_ref[...] += jnp.sum((gap * gap).reshape(tile // 8, 8, r), axis=0)


def fit_and_predict(system, features, targets, valid, ridge):
    n, f = features.shape
    r = targets.shape[1]
    smem, vmem = pl.BlockSpec(memory_space=pltpu.SMEM), pl.BlockSpec(memory_space=pltpu.VMEM)
    anywhere = pl.BlockSpec(memory_space=pl.ANY)
    return pl.pallas_call(
        functools.partial(fit_kernel, 512),
        in_specs=[smem, smem, vmem, anywhere, anywhere],
        out_specs=[vmem, vmem],
        out_shape=[jax.ShapeDtypeStruct((n, r), BF), jax.ShapeDtypeStruct((8, r), F32)],
        scratch_shapes=[
            pltpu.VMEM((f, f + r), F32),
            pltpu.VMEM((n, f), F32),
            pltpu.VMEM((n, r), F32),
            pltpu.SemaphoreType.DMA((2,)),
        ],
        compiler_params=pltpu.CompilerParams(vmem_limit_bytes=48 * 2**20),
        name="fit",
    )(valid, ridge, system, features, targets)


def prefix_kernel(part_ref, out_ref, twin_in, pair, row_in, mine, z_in, before, through, x_in, full, sends, arrivals):
    z, x, r = lax.axis_index("tm_0"), lax.axis_index("tm_1"), lax.axis_index("rows")
    y, core = r // 2, lax.rem(r, 2)
    twin = {"rows": r + 1 - 2 * core}
    f, width = part_ref.shape
    count, half, piece = f // B, B // 2, B // 8

    def other(i, d):
        return lax.rem(i + d, 4)

    barrier = pltpu.get_barrier_semaphore()
    pl.semaphore_signal(barrier, inc=1, device_id=twin, device_id_type=MESH)
    for d in (1, 2, 3):
        for peer in ({"rows": 2 * other(y, d) + core}, {"tm_0": other(z, d)}, {"tm_1": other(x, d)}):
            pl.semaphore_signal(barrier, inc=1, device_id=peer, device_id_type=MESH)
    pl.semaphore_wait(barrier, 10)

    def send(phase, j, d, src, dst, peer):
        at = (phase * count + j) * 3 + d - 1
        return pltpu.make_async_remote_copy(
            src_ref=src,
            dst_ref=dst,
            send_sem=sends.at[at],
            recv_sem=arrivals.at[at],
            device_id=peer,
            device_id_type=MESH,
        )

    def multiple(i):
        return pl.multiple_of(i, piece)

    def band(ref, j, start, size):
        return ref.at[pl.ds(multiple(j * B + start), size), pl.ds(j * B, width - j * B)]

    def small(ref, j, d=None):
        where = (pl.ds(j * piece, piece), pl.ds(j * B, width - j * B))
        return ref.at[where] if d is None else ref.at[(d - 1, *where)]

    def pair_rows(ref, j, start, size):
        return ref.at[pl.ds(multiple(j * half + start), size), pl.ds(j * B, width - j * B)]

    def to_twin(j):
        return send(0, j, 1, band(part_ref, j, half * (1 - core), half), pair_rows(twin_in, j, 0, half), twin)

    def to_row(j, d):
        to = other(y, d)
        return send(1, j, d, pair_rows(pair, j, piece * to, piece), small(row_in, j, d), {"rows": 2 * to + core})

    def to_z(j, d):
        return send(2, j, d, small(mine, j), small(z_in, j, d), {"tm_0": other(z, d)})

    def to_x(j, d, src):
        return send(3, j, d, small(src, j), small(x_in, j, d), {"tm_1": other(x, d)})

    def own(j):
        return band(full, j, half * core + piece * y, piece)

    def spread_row(j, d):
        return send(4, j, d, own(j), own(j), {"rows": 2 * other(y, d) + core})

    def row_arrival(j, d):
        there = band(full, j, half * core + piece * other(y, 4 - d), piece)
        return send(4, j, d, there, there, twin)

    def spread_twin(j):
        ours = band(full, j, half * core, half)
        return send(5, j, 1, ours, ours, twin)

    def twin_arrival(j):
        there = band(full, j, half * (1 - core), half)
        return send(5, j, 1, there, there, twin)

    def stage(p, j):
        if p == 0:
            to_twin(j).start()
        if p == 1:
            to_twin(j).wait_recv()
            pair_rows(pair, j, 0, half)[...] = (
                band(part_ref, j, half * core, half)[...] + pair_rows(twin_in, j, 0, half)[...]
            )
            for d in (1, 2, 3):
                to_row(j, d).start()
        if p == 2:
            total = pair_rows(pair, j, piece * y, piece)[...]
            for d in (1, 2, 3):
                to_row(j, d).wait_recv()
                total += small(row_in, j, d)[...]
            small(mine, j)[...] = total
            small(before, j)[...] = jnp.zeros_like(total)
            for d in (1, 2, 3):
                pl.when(z + d < 4)(lambda d=d: to_z(j, d).start())
        if p == 3:
            for d in (1, 2, 3):

                @pl.when(z >= d)
                def _(d=d):
                    to_z(j, d).wait_recv()
                    small(before, j)[...] += small(z_in, j, d)[...]

            small(through, j)[...] = small(before, j)[...] + small(mine, j)[...]
            for d in (1, 2, 3):
                pl.when(x + d < 4)(lambda d=d: to_x(j, d, through).start())
                pl.when(x + d >= 4)(lambda d=d: to_x(j, d, before).start())
        if p == 4:
            total = small(before, j)[...]
            for d in (1, 2, 3):
                to_x(j, d, before).wait_recv()
                total += small(x_in, j, d)[...]
            own(j)[...] = total
            for d in (1, 2, 3):
                spread_row(j, d).start()
        if p == 5:
            for d in (1, 2, 3):
                row_arrival(j, d).wait_recv()
            spread_twin(j).start()
        if p == 6:
            twin_arrival(j).wait_recv()
            band(out_ref, j, 0, B)[...] = band(full, j, 0, B)[...]

    for t in range(count + 6):
        for p in range(6, -1, -1):
            if 0 <= t - p < count:
                stage(p, t - p)
    for j in range(count):
        to_twin(j).wait_send()
        spread_twin(j).wait_send()
        for d in (1, 2, 3):
            to_row(j, d).wait_send()
            pl.when(z + d < 4)(lambda d=d: to_z(j, d).wait_send())
            to_x(j, d, before).wait_send()
            spread_row(j, d).wait_send()


def prefix_of_shards(part):
    f, width = part.shape
    count = f // B
    piece = (f // 8, width)
    return pl.pallas_call(
        prefix_kernel,
        in_specs=[pl.BlockSpec(memory_space=pltpu.VMEM)],
        out_specs=pl.BlockSpec(memory_space=pltpu.VMEM),
        out_shape=jax.ShapeDtypeStruct((f, width), F32),
        scratch_shapes=[
            pltpu.VMEM((f // 2, width), F32),
            pltpu.VMEM((f // 2, width), F32),
            pltpu.VMEM((3, *piece), F32),
            pltpu.VMEM(piece, F32),
            pltpu.VMEM((3, *piece), F32),
            pltpu.VMEM(piece, F32),
            pltpu.VMEM(piece, F32),
            pltpu.VMEM((3, *piece), F32),
            pltpu.VMEM((f, width), F32),
            pltpu.SemaphoreType.DMA((18 * count,)),
            pltpu.SemaphoreType.DMA((18 * count,)),
        ],
        compiler_params=pltpu.CompilerParams(
            collective_id=0, has_side_effects=True, vmem_limit_bytes=24 * 2**20
        ),
        name="prefix",
    )(part)


def body(features, targets, row_counts, ridge_codes):
    n = features.shape[0]
    shard = lax.axis_index(TM)
    counts = row_counts.astype(F32)
    valid = jnp.clip(row_counts[shard] - lax.axis_index("rows") * n, 0, n).reshape(1)
    system = gram_and_cross(features, targets, valid)
    system = prefix_of_shards(system)
    seen = jnp.sum(jnp.where(jnp.arange(counts.shape[0]) < shard, counts, 0.0))
    first = (shard == 0).astype(F32)
    ridge = ridge_codes[jnp.maximum(shard - 1, 0)].astype(F32) * seen / 16.0 + first
    forecast, errors = fit_and_predict(system, features, targets, valid, jnp.stack([ridge, 1.0 - first]))
    total = lax.psum(jnp.sum(errors), "rows")
    mse = total / (counts[shard] * targets.shape[1])
    return forecast, mse.reshape(1)


def solution(mesh):
    finer = Mesh(mesh.devices.reshape(4, 4, mesh.shape["rows"]), ("tm_0", "tm_1", "rows"))
    placed = (P(TM_ROWS, None), P(TM_ROWS, None), P(), P())
    return jax.shard_map(
        body, mesh=finer, in_specs=placed, out_specs=(P(TM_ROWS, None), P(TM)), check_vma=False
    )
```

time: 344 us -> 100 us (0.29); the launches traced: 338 us -> 98.9 us
  other arithmetic: 121 us -> 2.68 us
  matrix products: 77.4 us -> 0 us
  Pallas kernels: 0 us -> 73.4 us
  waiting for transfers between devices: 43.4 us -> 0 us
  blocking collectives: 45.2 us -> 12.5 us
  local copies, waits for them, and re-layouts: 24.3 us -> 5.28 us
  between operations: 21.7 us -> 5.11 us
  starting transfers between devices: 5.15 us -> 0 us
    another operation x18 -> x1, other arithmetic: 118 us -> 0.08 us  [body(): jnp.stack([ridge, 1.0 - first])]
    pallas_call x0 -> x3, Pallas kernels: none -> 73.4 us  [the longest x1 37.4 us: prefix_of_shards(): pl.pallas_call(prefix_kernel, in_specs=[pl.BlockSpec(memory_space=pltpu.V...]
    dot_general x3 -> x0, matrix products: 67.8 us -> none  [the longest x1 35.5 us: body(): lax.dot_general(weighted, features, contract_product, precision=lax.Preci...]
    all_gather x4 -> x0, blocking collectives: 37.6 us -> none  [prefix_by_axis(): pieces = jax.tree.map(lambda part: lax.all_gather(part, axis), so_far)]
    all_gather x1 -> x0, waiting for transfers between devices: 25.4 us -> none  [turned_gather(): out = lax.all_gather(both, axis, axis=0, tiled=True)]
    all_to_all x1 -> x0, waiting for transfers between devices: 17.9 us -> none  [summed_on_arrival(): lax.all_to_all(in_blocks(value, dim, count), axis, 0, 0, tiled=True)]
    psum x0 -> x1, blocking collectives: none -> 12.5 us  [body(): total = lax.psum(jnp.sum(errors), 'rows')]
    another operation x20 -> x0, matrix products: 9.6 us -> none  [the longest x14 7.27 us: ridge_solve(): return jax.scipy.linalg.cho_solve((lower_factor, True), cross_sum)]
  transfers between devices with their start and end apart: 2 -> 0, of which waited for: 2 -> 0; matrix products, arithmetic and copies ran while one was open for 2% -> 0% of each run, Pallas kernels for 0% -> 0%
where the time goes in v1:
time: 100 us; the launch traced here: 98.9 us
  Pallas kernels  73.4 us (73%)
  blocking collectives  12.5 us (12%)
  local copies, waits for them, and re-layouts  5.28 us (5%)
  between operations  5.11 us (5%)
  other arithmetic  2.68 us (3%)
    pallas_call x1, Pallas kernels, prefix_of_shards(): pl.pallas_call(prefix_kernel, in_specs=[pl.BlockSpec(memory_space=pltpu.V...  37.4 us
    pallas_call x1, Pallas kernels, fit_and_predict(): pl.pallas_call(functools.partial(fit_kernel, 512), in_specs=[smem, smem,...  20.5 us
    pallas_call x1, Pallas kernels, gram_and_cross(): pl.pallas_call(functools.partial(gram_kernel, tile), grid=(n // tile,), i...  15.5 us
    psum x1, blocking collectives, body(): total = lax.psum(jnp.sum(errors), 'rows')  12.5 us
    unnamed x4, local copies, waits for them, and re-layouts  2.19 us

profile of v1, /device:TPU:65, one launch (start us, length us, event | category | flops | bytes accessed | tf_op | source)
XLA Modules:
  0.0 98.9 jit_solution(14109797134933137647)
XLA Ops:
  0.6 1.3 %fusion = f32[]{:T(128)} fusion(s32[]{:T(128)S(6)} %add.14, s32[16]{0:T(128)} %param.6), kind=kLoop, calls=%fused_computation.1 | loop fusion | flops 63 | bytes 72 | tf_op jit(solution)/shard_map/reduce_sum | solution.py:417
  2.0 1.2 %dynamic_slice.9 = s32[1]{0:T(128)} dynamic-slice(s32[16]{0:T(128)} %param.6, s32[]{:T(128)S(6)} %select_n.9), dynamic_slice_sizes={1} | dynamic-slice | bytes 12 | tf_op jit(solution)/shard_map/dynamic_slice | solution.py:414
  3.9 1.3 %dynamic_slice.10 = s32[1]{0:T(128)} dynamic-slice(s32[16]{0:T(128)} %param.7, s32[]{:T(128)S(6)} %max.8), dynamic_slice_sizes={1} | dynamic-slice | bytes 12 | tf_op jit(solution)/shard_map/dynamic_slice | solution.py:419
  6.5 0.1 pad_maximum_fusion.ridge_ref
  6.6 0.7 convert_element_type.14
  7.2 0.6 dynamic_slice.11
  8.5 0.0 copy-start
  8.5 2.2 %copy-done = f32[8192,128]{1,0:T(8,128)S(1)} copy-done((f32[8192,128]{1,0:T(8,128)S(1)}, f32[8192,128]{1,0:T(8,128)}, u32[]{:S(2)}) %copy-start) | copy-done | bytes 4194328
  10.6 0.0 copy-start.1
  10.6 15.5 %gram.1.part_ref = f32[512,640]{1,0:T(8,128)S(1)} custom-call(s32[1]{0:T(128)} %bitcast.1.valid_ref, f32[8192,512]{1,0:T(8,128)} %x_hbm.1, f32[8192,128]{1,0:T(8,128)S(1)} %copy-done), custom_call_target="tpu_custom_call" | custom-call | tf_op jit(solution)/shard_map/gram/pallas_call | solution.py:85
  26.2 37.4 %prefix.1.system_ref = f32[512,640]{1,0:T(8,128)S(1)} custom-call(f32[512,640]{1,0:T(8,128)S(1)} %gram.1.part_ref), custom_call_target="tpu_custom_call" | custom-call | tf_op jit(solution)/shard_map/prefix/pallas_call | solution.py:385
  63.5 0.0 copy-done.1
  63.5 20.5 %fit.1 = (bf16[8192,128]{1,0:T(8,128)(2,1)}, f32[8,128]{1,0:T(8,128)S(1)}) custom-call(s32[1]{0:T(128)} %bitcast.1.valid_ref, f32[2]{0:T(128)S(1)} %pad_maximum_fusion.ridge_ref, f32[512,640]{1,0:T(8,128)S(1)} %prefix.1.system_ref, f32[8192,512]{1,0:T(8,128)} %x_hbm.1, f32[8192,128]{1,0:T(8,128)S(1)} %copy-done.1), custom_call_target="tpu_custom_call" | custom-call | tf_op jit(solution)/shard_map/fit/pallas_call | solution.py:232
  84.1 0.6 reduce_sum.19
  84.7 12.5 %psum.7 = f32[]{:T(128)} all-reduce(f32[]{:T(128)} %reduce_sum.19), channel_id=1, replica_groups=mesh['tm_0'=4,'tm_1'=4,'rows'=8] {'rows'}, use_global_device_ids=true, to_apply=%region_2.3 | all-reduce | flops 1 | bytes 8 | tf_op jit(solution)/shard_map/psum | solution.py:421
Async XLA Ops:
  8.5 2.2 %copy-start = (f32[8192,128]{1,0:T(8,128)S(1)}, f32[8192,128]{1,0:T(8,128)}, u32[]{:S(2)}) copy-start(f32[8192,128]{1,0:T(8,128)} %y_hbm.1) | copy-start | bytes 12582916
  10.6 52.9 %copy-start.1 = (f32[8192,128]{1,0:T(8,128)S(1)}, f32[8192,128]{1,0:T(8,128)}, u32[]{:S(2)}) copy-start(f32[8192,128]{1,0:T(8,128)} %y_hbm.1) | copy-start | bytes 12582916

commit v2 on v1

--- a/solution.py
+++ b/solution.py
@@ -34,6 +34,10 @@
     return lax.dot_general(left, right, contract, preferred_element_type=F32)
 
 
+def packed(i, j, f, width):
+    return sum(width - k * B for k in range(i)) + (j - i) * B
+
+
 def full_dot(a, b, dims=(1, 0)):
     ah, am, al = thirds_of(a)
     bh, bm, bl = thirds_of(b)
@@ -42,10 +46,19 @@
     return mxu(left, right, dims)
 
 
-def gram_kernel(tile, valid_ref, x_ref, y_ref, out_ref, upper, lower, turned):
+def shard_index():
+    return lax.axis_index("tm_0") * lax.axis_size("tm_1") + lax.axis_index("tm_1")
+
+
+def valid_here(counts_ref, rows):
+    return counts_ref[shard_index()] - lax.axis_index("rows") * rows
+
+
+def gram_kernel(tile, counts_ref, x_ref, y_ref, out_ref, upper, lower, turned):
     step = pl.program_id(0)
     f, r = x_ref.shape[1], y_ref.shape[1]
     half = f // 2
+    valid_rows = valid_here(counts_ref, tile * pl.num_programs(0))
 
     @pl.when(step == 0)
     def _():
@@ -53,7 +66,7 @@
             acc[...] = jnp.zeros_like(acc)
 
     rows = step * tile + lax.broadcasted_iota(jnp.int32, (tile, 1), 0)
-    valid = rows < valid_ref[0]
+    valid = rows < valid_rows
     xh, xl = halves_of(jnp.where(valid, x_ref[...], 0.0))
     yh, yl = halves_of(y_ref[...])
     upper[...] += mxu(xh[:, :half], jnp.concatenate([yh, yl, xl, xh], axis=1), (0, 0))
@@ -67,21 +80,24 @@
             return acc, pl.ds(i * B % half, B), 0 if i * B < half else half
 
         for i in range(f // B):
-            a = pl.ds(i * B, B)
             acc, here, skipped = strip(i)
             for j in range(i, f // B):
                 mirror, there, _ = strip(j)
-                b = pl.ds(j * B, B)
-                out_ref[a, b] = acc[here, pl.ds(2 * r + f + j * B - skipped, B)]
-                out_ref[a, b] += acc[here, pl.ds(2 * r + j * B, B)]
-                out_ref[a, b] += mirror[there, pl.ds(2 * r + i * B, B)].T
-            out_ref[a, pl.ds(f, r)] = acc[here, pl.ds(0, r)] + acc[here, pl.ds(r, r)] + turned[:, a].T
-
-
-def gram_and_cross(features, targets, valid):
+                b = pl.ds(packed(i, j, f, f + r), B)
+                out_ref[:, b] = acc[here, pl.ds(2 * r + f + j * B - skipped, B)]
+                out_ref[:, b] += acc[here, pl.ds(2 * r + j * B, B)]
+                out_ref[:, b] += mirror[there, pl.ds(2 * r + i * B, B)].T
+            b = pl.ds(packed(i, f // B, f, f + r), r)
+            out_ref[:, b] = acc[here, pl.ds(0, r)]
+            out_ref[:, b] += acc[here, pl.ds(r, r)]
+            out_ref[:, b] += turned[:, pl.ds(i * B, B)].T
+
+
+def gram_and_cross(features, targets, counts):
     n, f = features.shape
     r = targets.shape[1]
     tile = 1024
+    columns = packed(f // B, f // B, f, f + r)
     return pl.pallas_call(
         functools.partial(gram_kernel, tile),
         grid=(n // tile,),
@@ -90,16 +106,16 @@
             pl.BlockSpec((tile, f), lambda i: (i, 0)),
             pl.BlockSpec((tile, r), lambda i: (i, 0)),
         ],
-        out_specs=pl.BlockSpec((f, f + r), lambda i: (0, 0)),
-        out_shape=jax.ShapeDtypeStruct((f, f + r), F32),
+        out_specs=pl.BlockSpec((B, columns), lambda i: (0, 0)),
+        out_shape=jax.ShapeDtypeStruct((B, columns), F32),
         scratch_shapes=[
             pltpu.VMEM((f // 2, 2 * f + 2 * r), F32),
             pltpu.VMEM((f // 2, 3 * f // 2 + 2 * r), F32),
             pltpu.VMEM((r, f), F32),
         ],
-        compiler_params=pltpu.CompilerParams(vmem_limit_bytes=40 * 2**20),
+        compiler_params=pltpu.CompilerParams(vmem_limit_bytes=56 * 2**20),
         name="gram",
-    )(valid, features, targets)
+    )(counts, features, targets)
 
 
 def row_of(x, s):
@@ -193,7 +209,7 @@
         system[here, last] += full_dot(system[here, behind], system[behind, last])
 
 
-def fit_kernel(tile, valid_ref, ridge_ref, system_ref, x_hbm, y_hbm, out_ref, error_ref, system, x, y, sems):
+def fit_kernel(tile, counts_ref, codes_ref, system_ref, x_hbm, y_hbm, out_ref, error_ref, system, x, y, sems):
     n, f = x.shape
     r = y.shape[1]
     get_x = pltpu.make_async_copy(x_hbm, x, sems.at[0])
@@ -201,10 +217,17 @@
     get_x.start()
     get_y.start()
     for j in range(f // B):
-        upper = (pl.ds(j * B, B), pl.ds(j * B, f + r - j * B))
-        system[upper] = system_ref[upper]
-    solve_in_place(system, ridge_ref[0])
-    weights = -system[:, pl.ds(f, r)] * ridge_ref[1]
+        width = f + r - j * B
+        system[pl.ds(j * B, B), pl.ds(j * B, width)] = system_ref[:, pl.ds(packed(j, j, f, f + r), width)]
+    shard = shard_index()
+    seen = jnp.int32(0)
+    for k in range(counts_ref.shape[0]):
+        seen += jnp.where(k < shard, counts_ref[k], 0)
+    first = (shard == 0).astype(F32)
+    ridge = codes_ref[jnp.maximum(shard - 1, 0)].astype(F32) * seen.astype(F32) * 0.0625 + first
+    solve_in_place(system, ridge)
+    weights = -system[:, pl.ds(f, r)] * (1.0 - first)
+    valid_rows = valid_here(counts_ref, n)
     wh, wl = halves_of(weights)
     both = jnp.concatenate([wh, wl], axis=1)
     get_x.wait()
@@ -217,14 +240,14 @@
         xh, xl = halves_of(x[here, :])
         first = mxu(xh, both)
         value = first[:, :r] + first[:, r:] + mxu(xl, wh)
-        valid = i * tile + lax.broadcasted_iota(jnp.int32, (tile, r), 0) < valid_ref[0]
+        valid = i * tile + lax.broadcasted_iota(jnp.int32, (tile, r), 0) < valid_rows
         value = jnp.where(valid, value, 0.0)
         out_ref[here, :] = value.astype(BF)
         gap = jnp.where(valid, y[here, :] - value, 0.0)
         error_ref[...] += jnp.sum((gap * gap).reshape(tile // 8, 8, r), axis=0)
 
 
-def fit_and_predict(system, features, targets, valid, ridge):
+def fit_and_predict(system, features, targets, counts, codes):
     n, f = features.shape
     r = targets.shape[1]
     smem, vmem = pl.BlockSpec(memory_space=pltpu.SMEM), pl.BlockSpec(memory_space=pltpu.VMEM)
@@ -240,17 +263,16 @@
             pltpu.VMEM((n, r), F32),
             pltpu.SemaphoreType.DMA((2,)),
         ],
-        compiler_params=pltpu.CompilerParams(vmem_limit_bytes=48 * 2**20),
+        compiler_params=pltpu.CompilerParams(vmem_limit_bytes=56 * 2**20),
         name="fit",
-    )(valid, ridge, system, features, targets)
-
-
-def prefix_kernel(part_ref, out_ref, twin_in, pair, row_in, mine, z_in, before, through, x_in, full, sends, arrivals):
+    )(counts, codes, system, features, targets)
+
+
+def prefix_kernel(chunks, part_ref, out_ref, twin_in, pair, row_in, mine, z_in, before, through, x_in, full, sends, arrivals):
     z, x, r = lax.axis_index("tm_0"), lax.axis_index("tm_1"), lax.axis_index("rows")
     y, core = r // 2, lax.rem(r, 2)
     twin = {"rows": r + 1 - 2 * core}
-    f, width = part_ref.shape
-    count, half, piece = f // B, B // 2, B // 8
+    count, half, piece = len(chunks), B // 2, B // 8
 
     def other(i, d):
         return lax.rem(i + d, 4)
@@ -276,22 +298,20 @@
     def multiple(i):
         return pl.multiple_of(i, piece)
 
-    def band(ref, j, start, size):
-        return ref.at[pl.ds(multiple(j * B + start), size), pl.ds(j * B, width - j * B)]
+    def part(ref, j, start, size, d=None):
+        rows = pl.ds(start if isinstance(start, int) else multiple(start), size)
+        where = (rows, pl.ds(*chunks[j]))
+        return ref.at[where] if d is None else ref.at[(d - 1, *where)]
 
     def small(ref, j, d=None):
-        where = (pl.ds(j * piece, piece), pl.ds(j * B, width - j * B))
-        return ref.at[where] if d is None else ref.at[(d - 1, *where)]
-
-    def pair_rows(ref, j, start, size):
-        return ref.at[pl.ds(multiple(j * half + start), size), pl.ds(j * B, width - j * B)]
+        return part(ref, j, 0, piece, d)
 
     def to_twin(j):
-        return send(0, j, 1, band(part_ref, j, half * (1 - core), half), pair_rows(twin_in, j, 0, half), twin)
+        return send(0, j, 1, part(part_ref, j, half * (1 - core), half), part(twin_in, j, 0, half), twin)
 
     def to_row(j, d):
         to = other(y, d)
-        return send(1, j, d, pair_rows(pair, j, piece * to, piece), small(row_in, j, d), {"rows": 2 * to + core})
+        return send(1, j, d, part(pair, j, piece * to, piece), small(row_in, j, d), {"rows": 2 * to + core})
 
     def to_z(j, d):
         return send(2, j, d, small(mine, j), small(z_in, j, d), {"tm_0": other(z, d)})
@@ -300,21 +320,21 @@
         return send(3, j, d, small(src, j), small(x_in, j, d), {"tm_1": other(x, d)})
 
     def own(j):
-        return band(full, j, half * core + piece * y, piece)
+        return part(full, j, half * core + piece * y, piece)
 
     def spread_row(j, d):
         return send(4, j, d, own(j), own(j), {"rows": 2 * other(y, d) + core})
 
     def row_arrival(j, d):
-        there = band(full, j, half * core + piece * other(y, 4 - d), piece)
+        there = part(full, j, half * core + piece * other(y, 4 - d), piece)
         return send(4, j, d, there, there, twin)
 
     def spread_twin(j):
-        ours = band(full, j, half * core, half)
+        ours = part(full, j, half * core, half)
         return send(5, j, 1, ours, ours, twin)
 
     def twin_arrival(j):
-        there = band(full, j, half * (1 - core), half)
+        there = part(full, j, half * (1 - core), half)
         return send(5, j, 1, there, there, twin)
 
     def stage(p, j):
@@ -322,13 +342,13 @@
             to_twin(j).start()
         if p == 1:
             to_twin(j).wait_recv()
-            pair_rows(pair, j, 0, half)[...] = (
-                band(part_ref, j, half * core, half)[...] + pair_rows(twin_in, j, 0, half)[...]
+            part(pair, j, 0, half)[...] = (
+                part(part_ref, j, half * core, half)[...] + part(twin_in, j, 0, half)[...]
             )
             for d in (1, 2, 3):
                 to_row(j, d).start()
         if p == 2:
-            total = pair_rows(pair, j, piece * y, piece)[...]
+            total = part(pair, j, piece * y, piece)[...]
             for d in (1, 2, 3):
                 to_row(j, d).wait_recv()
                 total += small(row_in, j, d)[...]
@@ -362,7 +382,7 @@
             spread_twin(j).start()
         if p == 6:
             twin_arrival(j).wait_recv()
-            band(out_ref, j, 0, B)[...] = band(full, j, 0, B)[...]
+            part(out_ref, j, 0, B)[...] = part(full, j, 0, B)[...]
 
     for t in range(count + 6):
         for p in range(6, -1, -1):
@@ -378,25 +398,29 @@
             spread_row(j, d).wait_send()
 
 
-def prefix_of_shards(part):
-    f, width = part.shape
-    count = f // B
-    piece = (f // 8, width)
+CHUNKS = (640, 1152)
+
+
+def prefix_of_shards(value):
+    columns = value.shape[1]
+    chunks = [(sum(CHUNKS[:k]), w) for k, w in enumerate(CHUNKS)]
+    half, piece = (B // 2, columns), (B // 8, columns)
+    count = len(chunks)
     return pl.pallas_call(
-        prefix_kernel,
+        functools.partial(prefix_kernel, chunks),
         in_specs=[pl.BlockSpec(memory_space=pltpu.VMEM)],
         out_specs=pl.BlockSpec(memory_space=pltpu.VMEM),
-        out_shape=jax.ShapeDtypeStruct((f, width), F32),
+        out_shape=jax.ShapeDtypeStruct((B, columns), F32),
         scratch_shapes=[
-            pltpu.VMEM((f // 2, width), F32),
-            pltpu.VMEM((f // 2, width), F32),
+            pltpu.VMEM(half, F32),
+            pltpu.VMEM(half, F32),
             pltpu.VMEM((3, *piece), F32),
             pltpu.VMEM(piece, F32),
             pltpu.VMEM((3, *piece), F32),
             pltpu.VMEM(piece, F32),
             pltpu.VMEM(piece, F32),
             pltpu.VMEM((3, *piece), F32),
-            pltpu.VMEM((f, width), F32),
+            pltpu.VMEM((B, columns), F32),
             pltpu.SemaphoreType.DMA((18 * count,)),
             pltpu.SemaphoreType.DMA((18 * count,)),
         ],
@@ -404,23 +428,64 @@
             collective_id=0, has_side_effects=True, vmem_limit_bytes=24 * 2**20
         ),
         name="prefix",
-    )(part)
+    )(value)
+
+
+def error_kernel(targets, counts_ref, error_ref, out_ref, gathered, sends, arrivals):
+    r = lax.axis_index("rows")
+    size = lax.axis_size("rows")
+
+    def peer(d):
+        return {"rows": lax.rem(r + d, size)}
+
+    barrier = pltpu.get_barrier_semaphore()
+    for d in range(1, size):
+        pl.semaphore_signal(barrier, inc=1, device_id=peer(d), device_id_type=MESH)
+    pl.semaphore_wait(barrier, size - 1)
+    copies = [
+        pltpu.make_async_remote_copy(
+            src_ref=error_ref,
+            dst_ref=gathered.at[d - 1],
+            send_sem=sends.at[d - 1],
+            recv_sem=arrivals.at[d - 1],
+            device_id=peer(d),
+            device_id_type=MESH,
+        )
+        for d in range(1, size)
+    ]
+    for copy in copies:
+        copy.start()
+    total = error_ref[...]
+    for d, copy in enumerate(copies):
+        copy.wait_recv()
+        total += gathered[d]
+    out_ref[0] = jnp.sum(total) / (counts_ref[shard_index()].astype(F32) * targets)
+    for copy in copies:
+        copy.wait_send()
+
+
+def mean_error(errors, counts, targets):
+    size = lax.axis_size("rows")
+    smem, vmem = pl.BlockSpec(memory_space=pltpu.SMEM), pl.BlockSpec(memory_space=pltpu.VMEM)
+    return pl.pallas_call(
+        functools.partial(error_kernel, targets),
+        in_specs=[smem, vmem],
+        out_specs=smem,
+        out_shape=jax.ShapeDtypeStruct((1,), F32),
+        scratch_shapes=[
+            pltpu.VMEM((size - 1, *errors.shape), F32),
+            pltpu.SemaphoreType.DMA((size - 1,)),
+            pltpu.SemaphoreType.DMA((size - 1,)),
+        ],
+        compiler_params=pltpu.CompilerParams(collective_id=1, has_side_effects=True),
+        name="error",
+    )(counts, errors)
 
 
 def body(features, targets, row_counts, ridge_codes):
-    n = features.shape[0]
-    shard = lax.axis_index(TM)
-    counts = row_counts.astype(F32)
-    valid = jnp.clip(row_counts[shard] - lax.axis_index("rows") * n, 0, n).reshape(1)
-    system = gram_and_cross(features, targets, valid)
-    system = prefix_of_shards(system)
-    seen = jnp.sum(jnp.where(jnp.arange(counts.shape[0]) < shard, counts, 0.0))
-    first = (shard == 0).astype(F32)
-    ridge = ridge_codes[jnp.maximum(shard - 1, 0)].astype(F32) * seen / 16.0 + first
-    forecast, errors = fit_and_predict(system, features, targets, valid, jnp.stack([ridge, 1.0 - first]))
-    total = lax.psum(jnp.sum(errors), "rows")
-    mse = total / (counts[shard] * targets.shape[1])
-    return forecast, mse.reshape(1)
+    system = prefix_of_shards(gram_and_cross(features, targets, row_counts))
+    forecast, errors = fit_and_predict(system, features, targets, row_counts, ridge_codes)
+    return forecast, mean_error(errors, row_counts, targets.shape[1])
 
 
 def solution(mesh):

time: 100 us -> 82.3 us (0.82)
  blocking collectives: 12.5 us -> 0 us
  Pallas kernels: 73.4 us -> 77.4 us
  local copies, waits for them, and re-layouts: 5.28 us -> 2.09 us
  between operations: 5.11 us -> 2.42 us
  other arithmetic: 2.68 us -> 0 us
    psum x1 -> x0, blocking collectives: 12.5 us -> none  [body(): total = lax.psum(jnp.sum(errors), 'rows')]
    dynamic_slice x3 -> x0, local copies, waits for them, and re-layouts: 3.09 us -> none  [the longest x1 1.27 us: body(): ridge_codes[jnp.maximum(shard - 1, 0)].astype(F32) * seen / 16.0 + first]
    pallas_call x1 -> x2, Pallas kernels: 37.4 us -> 40 us  [the longest x1 33.5 us: prefix_of_shards(): pl.pallas_call(functools.partial(prefix_kernel, chunks), in_specs=[pl.Blo...]
    reduce_sum x2 -> x0, other arithmetic: 1.94 us -> none  [the longest x1 1.34 us: body(): seen = jnp.sum(jnp.where(jnp.arange(counts.shape[0]) < shard, counts, 0.0))]
where the time goes in v2:
time: 82.3 us; the launch traced here: 81.9 us
  Pallas kernels  77.4 us (94%)
  between operations  2.42 us (3%)
  local copies, waits for them, and re-layouts  2.09 us (3%)
    pallas_call x1, Pallas kernels, prefix_of_shards(): pl.pallas_call(functools.partial(prefix_kernel, chunks), in_specs=[pl.Blo...  33.5 us
    pallas_call x1, Pallas kernels, fit_and_predict(): pl.pallas_call(functools.partial(fit_kernel, 512), in_specs=[smem, smem,...  20.9 us
    pallas_call x1, Pallas kernels, gram_and_cross(): pl.pallas_call(functools.partial(gram_kernel, tile), grid=(n // tile,), i...  16.5 us
    pallas_call x1, Pallas kernels, mean_error(): pl.pallas_call(functools.partial(error_kernel, targets), in_specs=[smem,...  6.51 us
    unnamed x4, local copies, waits for them, and re-layouts  2.09 us

profile of v2, /device:TPU:65, one launch (start us, length us, event | category | flops | bytes accessed | tf_op | source)
XLA Modules:
  0.0 81.9 jit_solution(1495457333532087141)
XLA Ops:
  0.6 16.5 %gram.1.part_ref = f32[128,1792]{1,0:T(8,128)} custom-call(s32[16]{0:T(128)} %counts_ref.5, f32[8192,512]{1,0:T(8,128)} %x_hbm.1, f32[8192,128]{1,0:T(8,128)} %y_hbm.1), custom_call_target="tpu_custom_call" | custom-call | tf_op jit(solution)/shard_map/gram/pallas_call | solution.py:101
  17.1 0.0 copy-start.1
  17.1 1.2 %copy-done.1 = f32[128,1792]{1,0:T(8,128)S(1)} copy-done((f32[128,1792]{1,0:T(8,128)S(1)}, f32[128,1792]{1,0:T(8,128)}, u32[]{:S(2)}) %copy-start.1) | copy-done | bytes 917528
  18.3 33.5 %prefix.1.system_ref = f32[128,1792]{1,0:T(8,128)S(1)} custom-call(f32[128,1792]{1,0:T(8,128)S(1)} %copy-done.1), custom_call_target="tpu_custom_call" | custom-call | tf_op jit(solution)/shard_map/prefix/pallas_call | solution.py:409
  51.8 0.0 copy-start
  51.8 0.9 %copy-done = f32[128,1792]{1,0:T(8,128)} copy-done((f32[128,1792]{1,0:T(8,128)}, f32[128,1792]{1,0:T(8,128)S(1)}, u32[]{:S(2)}) %copy-start) | copy-done | bytes 917528
  52.7 20.9 %fit.1 = (bf16[8192,128]{1,0:T(8,128)(2,1)}, f32[8,128]{1,0:T(8,128)}) custom-call(s32[16]{0:T(128)} %counts_ref.5, s32[16]{0:T(128)} %codes_ref.1, f32[128,1792]{1,0:T(8,128)} %copy-done, f32[8192,512]{1,0:T(8,128)} %x_hbm.1, f32[8192,128]{1,0:T(8,128)} %y_hbm.1), custom_call_target="tpu_custom_call" | custom-call | tf_op jit(solution)/shard_map/fit/pallas_call | solution.py:255
  73.6 6.5 %error.1 = f32[1]{0:T(128)} custom-call(s32[16]{0:T(128)} %counts_ref.5, f32[8,128]{1,0:T(8,128)} %get-tuple-element.5.error_ref), custom_call_target="tpu_custom_call" | custom-call | tf_op jit(solution)/shard_map/error/pallas_call | solution.py:470
Async XLA Ops:
  17.1 1.2 %copy-start.1 = (f32[128,1792]{1,0:T(8,128)S(1)}, f32[128,1792]{1,0:T(8,128)}, u32[]{:S(2)}) copy-start(f32[128,1792]{1,0:T(8,128)} %gram.1.part_ref) | copy-start | bytes 2752516
  51.8 0.9 %copy-start = (f32[128,1792]{1,0:T(8,128)}, f32[128,1792]{1,0:T(8,128)S(1)}, u32[]{:S(2)}) copy-start(f32[128,1792]{1,0:T(8,128)S(1)} %prefix.1.system_ref) | copy-start | bytes 2752516

commit v3 on v2

--- a/solution.py
+++ b/solution.py
@@ -52,70 +52,6 @@
 
 def valid_here(counts_ref, rows):
     return counts_ref[shard_index()] - lax.axis_index("rows") * rows
-
-
-def gram_kernel(tile, counts_ref, x_ref, y_ref, out_ref, upper, lower, turned):
-    step = pl.program_id(0)
-    f, r = x_ref.shape[1], y_ref.shape[1]
-    half = f // 2
-    valid_rows = valid_here(counts_ref, tile * pl.num_programs(0))
-
-    @pl.when(step == 0)
-    def _():
-        for acc in (upper, lower, turned):
-            acc[...] = jnp.zeros_like(acc)
-
-    rows = step * tile + lax.broadcasted_iota(jnp.int32, (tile, 1), 0)
-    valid = rows < valid_rows
-    xh, xl = halves_of(jnp.where(valid, x_ref[...], 0.0))
-    yh, yl = halves_of(y_ref[...])
-    upper[...] += mxu(xh[:, :half], jnp.concatenate([yh, yl, xl, xh], axis=1), (0, 0))
-    lower[...] += mxu(xh[:, half:], jnp.concatenate([yh, yl, xl, xh[:, half:]], axis=1), (0, 0))
-    turned[...] += mxu(yh, xl, (0, 0))
-
-    @pl.when(step == pl.num_programs(0) - 1)
-    def _():
-        def strip(i):
-            acc = upper if i * B < half else lower
-            return acc, pl.ds(i * B % half, B), 0 if i * B < half else half
-
-        for i in range(f // B):
-            acc, here, skipped = strip(i)
-            for j in range(i, f // B):
-                mirror, there, _ = strip(j)
-                b = pl.ds(packed(i, j, f, f + r), B)
-                out_ref[:, b] = acc[here, pl.ds(2 * r + f + j * B - skipped, B)]
-                out_ref[:, b] += acc[here, pl.ds(2 * r + j * B, B)]
-                out_ref[:, b] += mirror[there, pl.ds(2 * r + i * B, B)].T
-            b = pl.ds(packed(i, f // B, f, f + r), r)
-            out_ref[:, b] = acc[here, pl.ds(0, r)]
-            out_ref[:, b] += acc[here, pl.ds(r, r)]
-            out_ref[:, b] += turned[:, pl.ds(i * B, B)].T
-
-
-def gram_and_cross(features, targets, counts):
-    n, f = features.shape
-    r = targets.shape[1]
-    tile = 1024
-    columns = packed(f // B, f // B, f, f + r)
-    return pl.pallas_call(
-        functools.partial(gram_kernel, tile),
-        grid=(n // tile,),
-        in_specs=[
-            pl.BlockSpec(memory_space=pltpu.SMEM),
-            pl.BlockSpec((tile, f), lambda i: (i, 0)),
-            pl.BlockSpec((tile, r), lambda i: (i, 0)),
-        ],
-        out_specs=pl.BlockSpec((B, columns), lambda i: (0, 0)),
-        out_shape=jax.ShapeDtypeStruct((B, columns), F32),
-        scratch_shapes=[
-            pltpu.VMEM((f // 2, 2 * f + 2 * r), F32),
-            pltpu.VMEM((f // 2, 3 * f // 2 + 2 * r), F32),
-            pltpu.VMEM((r, f), F32),
-        ],
-        compiler_params=pltpu.CompilerParams(vmem_limit_bytes=56 * 2**20),
-        name="gram",
-    )(counts, features, targets)
 
 
 def row_of(x, s):
@@ -253,7 +189,7 @@
     smem, vmem = pl.BlockSpec(memory_space=pltpu.SMEM), pl.BlockSpec(memory_space=pltpu.VMEM)
     anywhere = pl.BlockSpec(memory_space=pl.ANY)
     return pl.pallas_call(
-        functools.partial(fit_kernel, 512),
+        functools.partial(fit_kernel, 2048),
         in_specs=[smem, smem, vmem, anywhere, anywhere],
         out_specs=[vmem, vmem],
         out_shape=[jax.ShapeDtypeStruct((n, r), BF), jax.ShapeDtypeStruct((8, r), F32)],
@@ -268,7 +204,96 @@
     )(counts, codes, system, features, targets)
 
 
-def prefix_kernel(chunks, part_ref, out_ref, twin_in, pair, row_in, mine, z_in, before, through, x_in, full, sends, arrivals):
+def split_tile(i, tile, valid_rows, x, y, xh, xl, yh, yl):
+    here = pl.ds(pl.multiple_of(i * tile, tile), tile)
+    valid = i * tile + lax.broadcasted_iota(jnp.int32, (tile, 1), 0) < valid_rows
+    xh[here, :], xl[here, :] = halves_of(jnp.where(valid, x[here, :], 0.0))
+    yh[here, :], yl[here, :] = halves_of(y[here, :])
+
+
+def upper_products(i, tile, xh, xl, yh, yl, upper, mirror, turned):
+    here = pl.ds(pl.multiple_of(i * tile, tile), tile)
+    half = xh.shape[1] // 2
+    left, right = xh[here, :half], xh[here, half:]
+    low = xl[here, :]
+    high = yh[here, :]
+    upper[...] += mxu(left, jnp.concatenate([high, yl[here, :], low, left, right], axis=1), (0, 0))
+    mirror[...] += mxu(right, low[:, :half], (0, 0))
+    turned[...] += mxu(high, low, (0, 0))
+
+
+def lower_products(i, tile, xh, xl, yh, yl, lower):
+    here = pl.ds(pl.multiple_of(i * tile, tile), tile)
+    half = xh.shape[1] // 2
+    right = xh[here, half:]
+    lower[...] += mxu(right, jnp.concatenate([yh[here, :], yl[here, :], xl[here, half:], right], axis=1), (0, 0))
+
+
+def pack_upper(out, upper, mirror, turned, f, r):
+    half = f // 2
+    for i in range(half // B):
+        here = pl.ds(i * B, B)
+        for j in range(i, f // B):
+            b = pl.ds(packed(i, j, f, f + r), B)
+            out[:, b] = upper[here, pl.ds(2 * r + f + j * B, B)]
+            out[:, b] += upper[here, pl.ds(2 * r + j * B, B)]
+            other = upper if j * B < half else mirror
+            at = 2 * r if j * B < half else 0
+            out[:, b] += other[pl.ds(j * B % half, B), pl.ds(at + i * B, B)].T
+        pack_cross(out, i, upper, turned, f, r)
+
+
+def pack_lower(out, lower, turned, f, r):
+    half = f // 2
+    for i in range(half // B, f // B):
+        here = pl.ds(i * B - half, B)
+        for j in range(i, f // B):
+            b = pl.ds(packed(i, j, f, f + r), B)
+            out[:, b] = lower[here, pl.ds(2 * r + j * B, B)]
+            out[:, b] += lower[here, pl.ds(2 * r + j * B - half, B)]
+            out[:, b] += lower[pl.ds(j * B - half, B), pl.ds(2 * r + i * B - half, B)].T
+        pack_cross(out, i, lower, turned, f, r)
+
+
+def pack_cross(out, i, acc, turned, f, r):
+    here = pl.ds(i * B % (f // 2), B)
+    b = pl.ds(packed(i, f // B, f, f + r), r)
+    out[:, b] = acc[here, pl.ds(0, r)]
+    out[:, b] += acc[here, pl.ds(r, r)]
+    out[:, b] += turned[:, pl.ds(i * B, B)].T
+
+
+def prefix_kernel(
+    chunks,
+    tile,
+    counts_ref,
+    x_hbm,
+    y_hbm,
+    out_ref,
+    xf,
+    yf,
+    xh,
+    xl,
+    yh,
+    yl,
+    upper,
+    mirror,
+    lower,
+    turned,
+    part_ref,
+    twin_in,
+    pair,
+    row_in,
+    mine,
+    z_in,
+    before,
+    through,
+    x_in,
+    full,
+    loads,
+    sends,
+    arrivals,
+):
     z, x, r = lax.axis_index("tm_0"), lax.axis_index("tm_1"), lax.axis_index("rows")
     y, core = r // 2, lax.rem(r, 2)
     twin = {"rows": r + 1 - 2 * core}
@@ -282,7 +307,22 @@
     for d in (1, 2, 3):
         for peer in ({"rows": 2 * other(y, d) + core}, {"tm_0": other(z, d)}, {"tm_1": other(x, d)}):
             pl.semaphore_signal(barrier, inc=1, device_id=peer, device_id_type=MESH)
-    pl.semaphore_wait(barrier, 10)
+    def load(i):
+        here = pl.ds(pl.multiple_of(i * tile, tile), tile)
+        return (
+            pltpu.make_async_copy(x_hbm.at[here], xf.at[here], loads.at[2 * i]),
+            pltpu.make_async_copy(y_hbm.at[here], yf.at[here], loads.at[2 * i + 1]),
+        )
+
+    n, f = xf.shape
+    targets = yf.shape[1]
+    tiles = n // tile
+    for i in range(tiles):
+        for copy in load(i):
+            copy.start()
+    valid_rows = valid_here(counts_ref, n)
+    for acc in (upper, mirror, lower, turned):
+        acc[...] = jnp.zeros_like(acc)
 
     def send(phase, j, d, src, dst, peer):
         at = (phase * count + j) * 3 + d - 1
@@ -384,10 +424,40 @@
             twin_arrival(j).wait_recv()
             part(out_ref, j, 0, B)[...] = part(full, j, 0, B)[...]
 
-    for t in range(count + 6):
-        for p in range(6, -1, -1):
-            if 0 <= t - p < count:
-                stage(p, t - p)
+    def split(i):
+        for copy in load(i):
+            copy.wait()
+        split_tile(i, tile, valid_rows, xf, yf, xh, xl, yh, yl)
+
+    split(0)
+
+    @pl.loop(1, tiles)
+    def _(i):
+        upper_products(i - 1, tile, xh, xl, yh, yl, upper, mirror, turned)
+        split(i)
+
+    upper_products(tiles - 1, tile, xh, xl, yh, yl, upper, mirror, turned)
+    pack_upper(part_ref, upper, mirror, turned, f, targets)
+    pl.semaphore_wait(barrier, 10)
+    stage(0, 0)
+    early = 2
+
+    @pl.loop(0, early)
+    def _(i):
+        lower_products(i, tile, xh, xl, yh, yl, lower)
+
+    stage(1, 0)
+
+    @pl.loop(early, tiles)
+    def _(i):
+        lower_products(i, tile, xh, xl, yh, yl, lower)
+
+    pack_lower(part_ref, lower, turned, f, targets)
+    stage(0, 1)
+    for p in range(2, 7):
+        stage(p, 0)
+        stage(p - 1, 1)
+    stage(6, 1)
     for j in range(count):
         to_twin(j).wait_send()
         spread_twin(j).wait_send()
@@ -398,22 +468,33 @@
             spread_row(j, d).wait_send()
 
 
-CHUNKS = (640, 1152)
-
-
-def prefix_of_shards(value):
-    columns = value.shape[1]
-    chunks = [(sum(CHUNKS[:k]), w) for k, w in enumerate(CHUNKS)]
-    half, piece = (B // 2, columns), (B // 8, columns)
-    count = len(chunks)
+def prefix_of_shards(features, targets, counts):
+    n, f = features.shape
+    r = targets.shape[1]
+    half, tile = f // 2, 1024
+    first, columns = packed(half // B, half // B, f, f + r), packed(f // B, f // B, f, f + r)
+    chunks = [(0, first), (first, columns - first)]
+    pair, piece = (B // 2, columns), (B // 8, columns)
+    anywhere = pl.BlockSpec(memory_space=pl.ANY)
     return pl.pallas_call(
-        functools.partial(prefix_kernel, chunks),
-        in_specs=[pl.BlockSpec(memory_space=pltpu.VMEM)],
+        functools.partial(prefix_kernel, chunks, tile),
+        in_specs=[pl.BlockSpec(memory_space=pltpu.SMEM), anywhere, anywhere],
         out_specs=pl.BlockSpec(memory_space=pltpu.VMEM),
         out_shape=jax.ShapeDtypeStruct((B, columns), F32),
         scratch_shapes=[
-            pltpu.VMEM(half, F32),
-            pltpu.VMEM(half, F32),
+            pltpu.VMEM((n, f), F32),
+            pltpu.VMEM((n, r), F32),
+            pltpu.VMEM((n, f), BF),
+            pltpu.VMEM((n, f), BF),
+            pltpu.VMEM((n, r), BF),
+            pltpu.VMEM((n, r), BF),
+            pltpu.VMEM((half, 2 * f + 2 * r), F32),
+            pltpu.VMEM((half, half), F32),
+            pltpu.VMEM((half, f + 2 * r), F32),
+            pltpu.VMEM((r, f), F32),
+            pltpu.VMEM((B, columns), F32),
+            pltpu.VMEM(pair, F32),
+            pltpu.VMEM(pair, F32),
             pltpu.VMEM((3, *piece), F32),
             pltpu.VMEM(piece, F32),
             pltpu.VMEM((3, *piece), F32),
@@ -421,14 +502,15 @@
             pltpu.VMEM(piece, F32),
             pltpu.VMEM((3, *piece), F32),
             pltpu.VMEM((B, columns), F32),
-            pltpu.SemaphoreType.DMA((18 * count,)),
-            pltpu.SemaphoreType.DMA((18 * count,)),
+            pltpu.SemaphoreType.DMA((2 * n // tile,)),
+            pltpu.SemaphoreType.DMA((18 * len(chunks),)),
+            pltpu.SemaphoreType.DMA((18 * len(chunks),)),
         ],
         compiler_params=pltpu.CompilerParams(
-            collective_id=0, has_side_effects=True, vmem_limit_bytes=24 * 2**20
+            collective_id=0, has_side_effects=True, vmem_limit_bytes=58 * 2**20
         ),
         name="prefix",
-    )(value)
+    )(counts, features, targets)
 
 
 def error_kernel(targets, counts_ref, error_ref, out_ref, gathered, sends, arrivals):
@@ -483,7 +565,7 @@
 
 
 def body(features, targets, row_counts, ridge_codes):
-    system = prefix_of_shards(gram_and_cross(features, targets, row_counts))
+    system = prefix_of_shards(features, targets, row_counts)
     forecast, errors = fit_and_predict(system, features, targets, row_counts, ridge_codes)
     return forecast, mean_error(errors, row_counts, targets.shape[1])
 

time: 82.3 us -> 76.7 us (0.932)
  Pallas kernels: 77.4 us -> 74.2 us
  local copies, waits for them, and re-layouts: 2.09 us -> 0 us
    pallas_call x3 -> x2, Pallas kernels: 70.9 us -> 67.6 us  [the longest x1 48.8 us: prefix_of_shards(): pl.pallas_call(functools.partial(prefix_kernel, chunks, tile), in_specs=[...]
    unnamed x4 -> x0, local copies, waits for them, and re-layouts: 2.09 us -> none
where the time goes in v3:
time: 76.7 us; the launch traced here: 76.5 us
  Pallas kernels  74.2 us (97%)
  between operations  2.34 us (3%)
    pallas_call x1, Pallas kernels, prefix_of_shards(): pl.pallas_call(functools.partial(prefix_kernel, chunks, tile), in_specs=[...  48.8 us
    pallas_call x1, Pallas kernels, fit_and_predict(): pl.pallas_call(functools.partial(fit_kernel, 2048), in_specs=[smem, smem,...  18.9 us
    pallas_call x1, Pallas kernels, mean_error(): pl.pallas_call(functools.partial(error_kernel, targets), in_specs=[smem,...  6.52 us

profile of v3, /device:TPU:65, one launch (start us, length us, event | category | flops | bytes accessed | tf_op | source)
XLA Modules:
  0.0 76.5 jit_solution(17985171499429808050)
XLA Ops:
  0.6 48.8 %prefix.1.system_ref = f32[128,1792]{1,0:T(8,128)} custom-call(s32[16]{0:T(128)} %counts_ref.5, f32[8192,512]{1,0:T(8,128)} %x_hbm.3, f32[8192,128]{1,0:T(8,128)} %y_hbm.3), custom_call_target="tpu_custom_call" | custom-call | tf_op jit(solution)/shard_map/prefix/pallas_call | solution.py:479
  49.4 18.9 %fit.1 = (bf16[8192,128]{1,0:T(8,128)(2,1)}, f32[8,128]{1,0:T(8,128)}) custom-call(s32[16]{0:T(128)} %counts_ref.5, s32[16]{0:T(128)} %codes_ref.1, f32[128,1792]{1,0:T(8,128)} %prefix.1.system_ref, f32[8192,512]{1,0:T(8,128)} %x_hbm.3, f32[8192,128]{1,0:T(8,128)} %y_hbm.3), custom_call_target="tpu_custom_call" | custom-call | tf_op jit(solution)/shard_map/fit/pallas_call | solution.py:191
  68.3 6.5 %error.1 = f32[1]{0:T(128)} custom-call(s32[16]{0:T(128)} %counts_ref.5, f32[8,128]{1,0:T(8,128)} %get-tuple-element.5.error_ref), custom_call_target="tpu_custom_call" | custom-call | tf_op jit(solution)/shard_map/error/pallas_call | solution.py:552

commit v4 on v3

--- a/solution.py
+++ b/solution.py
@@ -123,91 +123,47 @@
     return jnp.concatenate(block, axis=0)
 
 
-def solve_in_place(system, ridge):
+def solve(rows_of, system, scaled, ridge):
     f, width = system.shape
     count = f // B
     diagonal = lax.broadcasted_iota(jnp.int32, (B, B), 0) == lax.broadcasted_iota(jnp.int32, (B, B), 1)
-    for j in range(count):
-        here = pl.ds(j * B, B)
+    for k in range(count):
+        here, part = pl.ds(k * B, B), pl.ds(k * B, width - k * B)
+        system[here, part] = rows_of(k)
+        if k:
+            earlier = pl.ds(0, k * B)
+            system[here, part] += full_dot(system[earlier, here], scaled[earlier, part], (0, 0))
         block = system[here, here] + jnp.where(diagonal, ridge, 0.0)
         inverse = negative_inverse([block[8 * i : 8 * i + 8, :] for i in range(B // 8)])
-        rest = system[here, pl.ds((j + 1) * B, width - (j + 1) * B)]
-        turned = full_dot(inverse, rest)
-        system[here, pl.ds((j + 1) * B, width - (j + 1) * B)] = turned
-        for k in range(j + 1, count):
-            at = (k - j - 1) * B
-            part = pl.ds(k * B, width - k * B)
-            system[pl.ds(k * B, B), part] += full_dot(rest[:, at : at + B], turned[:, at:], (0, 0))
+        rest = pl.ds((k + 1) * B, width - (k + 1) * B)
+        scaled[here, rest] = full_dot(inverse, system[here, rest])
     last = pl.ds(f, width - f)
     for j in range(count - 2, -1, -1):
-        here = pl.ds(j * B, B)
-        behind = pl.ds((j + 1) * B, f - (j + 1) * B)
-        system[here, last] += full_dot(system[here, behind], system[behind, last])
-
-
-def fit_kernel(tile, counts_ref, codes_ref, system_ref, x_hbm, y_hbm, out_ref, error_ref, system, x, y, sems):
-    n, f = x.shape
-    r = y.shape[1]
-    get_x = pltpu.make_async_copy(x_hbm, x, sems.at[0])
-    get_y = pltpu.make_async_copy(y_hbm, y, sems.at[1])
-    get_x.start()
-    get_y.start()
-    for j in range(f // B):
-        width = f + r - j * B
-        system[pl.ds(j * B, B), pl.ds(j * B, width)] = system_ref[:, pl.ds(packed(j, j, f, f + r), width)]
-    shard = shard_index()
-    seen = jnp.int32(0)
-    for k in range(counts_ref.shape[0]):
-        seen += jnp.where(k < shard, counts_ref[k], 0)
-    first = (shard == 0).astype(F32)
-    ridge = codes_ref[jnp.maximum(shard - 1, 0)].astype(F32) * seen.astype(F32) * 0.0625 + first
-    solve_in_place(system, ridge)
-    weights = -system[:, pl.ds(f, r)] * (1.0 - first)
-    valid_rows = valid_here(counts_ref, n)
-    wh, wl = halves_of(weights)
+        here, behind = pl.ds(j * B, B), pl.ds((j + 1) * B, f - (j + 1) * B)
+        scaled[here, last] += full_dot(scaled[here, behind], scaled[behind, last])
+
+
+def predict(tile, solution_part, scale, valid_rows, xh, xl, y, out_ref, error):
+    n, r = y.shape
+    wh, wl = halves_of(solution_part * scale)
     both = jnp.concatenate([wh, wl], axis=1)
-    get_x.wait()
-    get_y.wait()
-    error_ref[...] = jnp.zeros_like(error_ref)
+    error[...] = jnp.zeros_like(error)
 
     @pl.loop(0, n // tile)
     def _(i):
         here = pl.ds(pl.multiple_of(i * tile, tile), tile)
-        xh, xl = halves_of(x[here, :])
-        first = mxu(xh, both)
-        value = first[:, :r] + first[:, r:] + mxu(xl, wh)
+        first = mxu(xh[here, :], both)
+        value = first[:, :r] + first[:, r:] + mxu(xl[here, :], wh)
+        out_ref[here, :] = value.astype(BF)
         valid = i * tile + lax.broadcasted_iota(jnp.int32, (tile, r), 0) < valid_rows
-        value = jnp.where(valid, value, 0.0)
-        out_ref[here, :] = value.astype(BF)
         gap = jnp.where(valid, y[here, :] - value, 0.0)
-        error_ref[...] += jnp.sum((gap * gap).reshape(tile // 8, 8, r), axis=0)
-
-
-def fit_and_predict(system, features, targets, counts, codes):
-    n, f = features.shape
-    r = targets.shape[1]
-    smem, vmem = pl.BlockSpec(memory_space=pltpu.SMEM), pl.BlockSpec(memory_space=pltpu.VMEM)
-    anywhere = pl.BlockSpec(memory_space=pl.ANY)
-    return pl.pallas_call(
-        functools.partial(fit_kernel, 2048),
-        in_specs=[smem, smem, vmem, anywhere, anywhere],
-        out_specs=[vmem, vmem],
-        out_shape=[jax.ShapeDtypeStruct((n, r), BF), jax.ShapeDtypeStruct((8, r), F32)],
-        scratch_shapes=[
-            pltpu.VMEM((f, f + r), F32),
-            pltpu.VMEM((n, f), F32),
-            pltpu.VMEM((n, r), F32),
-            pltpu.SemaphoreType.DMA((2,)),
-        ],
-        compiler_params=pltpu.CompilerParams(vmem_limit_bytes=56 * 2**20),
-        name="fit",
-    )(counts, codes, system, features, targets)
+        error[...] += jnp.sum((gap * gap).reshape(tile // 8, 8, r), axis=0)
 
 
 def split_tile(i, tile, valid_rows, x, y, xh, xl, yh, yl):
     here = pl.ds(pl.multiple_of(i * tile, tile), tile)
     valid = i * tile + lax.broadcasted_iota(jnp.int32, (tile, 1), 0) < valid_rows
-    xh[here, :], xl[here, :] = halves_of(jnp.where(valid, x[here, :], 0.0))
+    xh[here, :], xl[here, :] = halves_of(jnp.where(valid, x[...], 0.0))
     yh[here, :], yl[here, :] = halves_of(y[here, :])
 
 
@@ -263,13 +219,15 @@
     out[:, b] += turned[:, pl.ds(i * B, B)].T
 
 
-def prefix_kernel(
+def backtest_kernel(
     chunks,
     tile,
     counts_ref,
+    codes_ref,
     x_hbm,
     y_hbm,
     out_ref,
+    mse_ref,
     xf,
     yf,
     xh,
@@ -290,9 +248,15 @@
     through,
     x_in,
     full,
+    system,
+    scaled,
+    error,
+    errors_in,
     loads,
     sends,
     arrivals,
+    error_sends,
+    error_arrivals,
 ):
     z, x, r = lax.axis_index("tm_0"), lax.axis_index("tm_1"), lax.axis_index("rows")
     y, core = r // 2, lax.rem(r, 2)
@@ -303,21 +267,24 @@
         return lax.rem(i + d, 4)
 
     barrier = pltpu.get_barrier_semaphore()
-    pl.semaphore_signal(barrier, inc=1, device_id=twin, device_id_type=MESH)
+    size = lax.axis_size("rows")
+    neighbours = [{"rows": lax.rem(r + d, size)} for d in range(1, size)]
     for d in (1, 2, 3):
-        for peer in ({"rows": 2 * other(y, d) + core}, {"tm_0": other(z, d)}, {"tm_1": other(x, d)}):
-            pl.semaphore_signal(barrier, inc=1, device_id=peer, device_id_type=MESH)
+        neighbours += [{"tm_0": other(z, d)}, {"tm_1": other(x, d)}]
+    for peer in neighbours:
+        pl.semaphore_signal(barrier, inc=1, device_id=peer, device_id_type=MESH)
     def load(i):
         here = pl.ds(pl.multiple_of(i * tile, tile), tile)
         return (
-            pltpu.make_async_copy(x_hbm.at[here], xf.at[here], loads.at[2 * i]),
+            pltpu.make_async_copy(x_hbm.at[here], xf.at[lax.rem(i, slots)], loads.at[2 * i]),
             pltpu.make_async_copy(y_hbm.at[here], yf.at[here], loads.at[2 * i + 1]),
         )
 
-    n, f = xf.shape
+    n, f = xh.shape
+    slots = xf.shape[0]
     targets = yf.shape[1]
     tiles = n // tile
-    for i in range(tiles):
+    for i in range(slots):
         for copy in load(i):
             copy.start()
     valid_rows = valid_here(counts_ref, n)
@@ -422,23 +389,27 @@
             spread_twin(j).start()
         if p == 6:
             twin_arrival(j).wait_recv()
-            part(out_ref, j, 0, B)[...] = part(full, j, 0, B)[...]
 
     def split(i):
         for copy in load(i):
             copy.wait()
-        split_tile(i, tile, valid_rows, xf, yf, xh, xl, yh, yl)
+        split_tile(i, tile, valid_rows, xf.at[lax.rem(i, slots)], yf, xh, xl, yh, yl)
 
     split(0)
 
     @pl.loop(1, tiles)
     def _(i):
+        @pl.when(i + slots - 1 < tiles)
+        def _():
+            for copy in load(i + slots - 1):
+                copy.start()
+
         upper_products(i - 1, tile, xh, xl, yh, yl, upper, mirror, turned)
         split(i)
 
     upper_products(tiles - 1, tile, xh, xl, yh, yl, upper, mirror, turned)
     pack_upper(part_ref, upper, mirror, turned, f, targets)
-    pl.semaphore_wait(barrier, 10)
+    pl.semaphore_wait(barrier, len(neighbours))
     stage(0, 0)
     early = 2
 
@@ -454,10 +425,51 @@
 
     pack_lower(part_ref, lower, turned, f, targets)
     stage(0, 1)
-    for p in range(2, 7):
+    for p in range(2, 6):
         stage(p, 0)
         stage(p - 1, 1)
-    stage(6, 1)
+    stage(6, 0)
+
+    shard = shard_index()
+    seen = jnp.int32(0)
+    for k in range(counts_ref.shape[0]):
+        seen += jnp.where(k < shard, counts_ref[k], 0)
+    first = (shard == 0).astype(F32)
+    ridge = codes_ref[jnp.maximum(shard - 1, 0)].astype(F32) * seen.astype(F32) * 0.0625 + first
+    columns = f + targets
+
+    def rows_of(k):
+        if k == 1:
+            stage(5, 1)
+        if 2 * k * B == f:
+            stage(6, 1)
+        return full[:, pl.ds(packed(k, k, f, columns), columns - k * B)]
+
+    solve(rows_of, system, scaled, ridge)
+    predict(2 * tile, scaled[:, pl.ds(f, targets)], first - 1.0, valid_rows, xh, xl, yf, out_ref, error)
+
+    errors_in[r] = error[...]
+
+    def send_error(d, slot):
+        return pltpu.make_async_remote_copy(
+            src_ref=error,
+            dst_ref=errors_in.at[slot],
+            send_sem=error_sends.at[d - 1],
+            recv_sem=error_arrivals.at[d - 1],
+            device_id=neighbours[d - 1],
+            device_id_type=MESH,
+        )
+
+    for d in range(1, size):
+        send_error(d, r).start()
+    for d in range(1, size):
+        send_error(d, lax.rem(r + size - d, size)).wait_recv()
+    total = errors_in[0]
+    for k in range(1, size):
+        total += errors_in[k]
+    mse_ref[0] = jnp.sum(total) / (counts_ref[shard].astype(F32) * targets)
+    for d in range(1, size):
+        send_error(d, r).wait_send()
     for j in range(count):
         to_twin(j).wait_send()
         spread_twin(j).wait_send()
@@ -468,21 +480,22 @@
             spread_row(j, d).wait_send()
 
 
-def prefix_of_shards(features, targets, counts):
+def backtest(features, targets, counts, codes):
     n, f = features.shape
     r = targets.shape[1]
     half, tile = f // 2, 1024
     first, columns = packed(half // B, half // B, f, f + r), packed(f // B, f // B, f, f + r)
     chunks = [(0, first), (first, columns - first)]
     pair, piece = (B // 2, columns), (B // 8, columns)
-    anywhere = pl.BlockSpec(memory_space=pl.ANY)
+    size = lax.axis_size("rows")
+    smem, anywhere = pl.BlockSpec(memory_space=pltpu.SMEM), pl.BlockSpec(memory_space=pl.ANY)
     return pl.pallas_call(
-        functools.partial(prefix_kernel, chunks, tile),
-        in_specs=[pl.BlockSpec(memory_space=pltpu.SMEM), anywhere, anywhere],
-        out_specs=pl.BlockSpec(memory_space=pltpu.VMEM),
-        out_shape=jax.ShapeDtypeStruct((B, columns), F32),
+        functools.partial(backtest_kernel, chunks, tile),
+        in_specs=[smem, smem, anywhere, anywhere],
+        out_specs=[pl.BlockSpec(memory_space=pltpu.VMEM), smem],
+        out_shape=[jax.ShapeDtypeStruct((n, r), BF), jax.ShapeDtypeStruct((1,), F32)],
         scratch_shapes=[
-            pltpu.VMEM((n, f), F32),
+            pltpu.VMEM((4, tile, f), F32),
             pltpu.VMEM((n, r), F32),
             pltpu.VMEM((n, f), BF),
             pltpu.VMEM((n, f), BF),
@@ -502,72 +515,25 @@
             pltpu.VMEM(piece, F32),
             pltpu.VMEM((3, *piece), F32),
             pltpu.VMEM((B, columns), F32),
+            pltpu.VMEM((f, f + r), F32),
+            pltpu.VMEM((f, f + r), F32),
+            pltpu.VMEM((8, r), F32),
+            pltpu.VMEM((size, 8, r), F32),
             pltpu.SemaphoreType.DMA((2 * n // tile,)),
             pltpu.SemaphoreType.DMA((18 * len(chunks),)),
             pltpu.SemaphoreType.DMA((18 * len(chunks),)),
-        ],
-        compiler_params=pltpu.CompilerParams(
-            collective_id=0, has_side_effects=True, vmem_limit_bytes=58 * 2**20
-        ),
-        name="prefix",
-    )(counts, features, targets)
-
-
-def error_kernel(targets, counts_ref, error_ref, out_ref, gathered, sends, arrivals):
-    r = lax.axis_index("rows")
-    size = lax.axis_size("rows")
-
-    def peer(d):
-        return {"rows": lax.rem(r + d, size)}
-
-    barrier = pltpu.get_barrier_semaphore()
-    for d in range(1, size):
-        pl.semaphore_signal(barrier, inc=1, device_id=peer(d), device_id_type=MESH)
-    pl.semaphore_wait(barrier, size - 1)
-    copies = [
-        pltpu.make_async_remote_copy(
-            src_ref=error_ref,
-            dst_ref=gathered.at[d - 1],
-            send_sem=sends.at[d - 1],
-            recv_sem=arrivals.at[d - 1],
-            device_id=peer(d),
-            device_id_type=MESH,
-        )
-        for d in range(1, size)
-    ]
-    for copy in copies:
-        copy.start()
-    total = error_ref[...]
-    for d, copy in enumerate(copies):
-        copy.wait_recv()
-        total += gathered[d]
-    out_ref[0] = jnp.sum(total) / (counts_ref[shard_index()].astype(F32) * targets)
-    for copy in copies:
-        copy.wait_send()
-
-
-def mean_error(errors, counts, targets):
-    size = lax.axis_size("rows")
-    smem, vmem = pl.BlockSpec(memory_space=pltpu.SMEM), pl.BlockSpec(memory_space=pltpu.VMEM)
-    return pl.pallas_call(
-        functools.partial(error_kernel, targets),
-        in_specs=[smem, vmem],
-        out_specs=smem,
-        out_shape=jax.ShapeDtypeStruct((1,), F32),
-        scratch_shapes=[
-            pltpu.VMEM((size - 1, *errors.shape), F32),
             pltpu.SemaphoreType.DMA((size - 1,)),
             pltpu.SemaphoreType.DMA((size - 1,)),
         ],
-        compiler_params=pltpu.CompilerParams(collective_id=1, has_side_effects=True),
-        name="error",
-    )(counts, errors)
+        compiler_params=pltpu.CompilerParams(
+            collective_id=0, has_side_effects=True, vmem_limit_bytes=51 * 2**20
+        ),
+        name="backtest",
+    )(counts, codes, features, targets)
 
 
 def body(features, targets, row_counts, ridge_codes):
-    system = prefix_of_shards(features, targets, row_counts)
-    forecast, errors = fit_and_predict(system, features, targets, row_counts, ridge_codes)
-    return forecast, mean_error(errors, row_counts, targets.shape[1])
+    return tuple(backtest(features, targets, row_counts, ridge_codes))
 
 
 def solution(mesh):

time: 76.7 us -> 68.9 us (0.90)
  Pallas kernels: 74.2 us -> 63.8 us
  local copies, waits for them, and re-layouts: 0 us -> 2.62 us
    pallas_call x3 -> x1, Pallas kernels: 74.2 us -> 63.8 us  [backtest(): pl.pallas_call(functools.partial(backtest_kernel, chunks, tile), in_specs...]
    unnamed x0 -> x5, local copies, waits for them, and re-layouts: none -> 2.62 us
where the time goes in v4:
time: 68.9 us; the launch traced here: 68.8 us
  Pallas kernels  63.8 us (93%)
  local copies, waits for them, and re-layouts  2.62 us (4%)
  between operations  2.41 us (3%)
    pallas_call x1, Pallas kernels, backtest(): pl.pallas_call(functools.partial(backtest_kernel, chunks, tile), in_specs...  63.8 us
    unnamed x5, local copies, waits for them, and re-layouts  2.62 us

profile of v4, /device:TPU:65, one launch (start us, length us, event | category | flops | bytes accessed | tf_op | source)
XLA Modules:
  0.0 68.8 jit_solution(13993656152036796732)
XLA Ops:
  0.6 0.0 copy-start
  0.6 0.6 copy-done
  1.3 0.0 copy-start.1
  1.3 0.7 copy-done.1
  1.9 63.8 %backtest.1 = (bf16[8192,128]{1,0:T(8,128)(2,1)S(1)}, f32[1]{0:T(128)}) custom-call(s32[16]{0:T(128)S(1)} %copy-done, s32[16]{0:T(128)S(1)} %copy-done.1, f32[8192,512]{1,0:T(8,128)} %x_hbm.1, f32[8192,128]{1,0:T(8,128)} %y_hbm.1), custom_call_target="tpu_custom_call" | custom-call | tf_op jit(solution)/shard_map/backtest/pallas_call | solution.py:492
  65.7 1.3 %copy.8 = bf16[8192,128]{1,0:T(8,128)(2,1)} copy(bf16[8192,128]{1,0:T(8,128)(2,1)S(1)} %get-tuple-element.4) | data formatting | bytes 4194304
Async XLA Ops:
  0.6 0.7 copy-start
  1.3 0.7 copy-start.1

commit v5 on v4

--- a/solution.py
+++ b/solution.py
@@ -151,7 +151,7 @@
 
     @pl.loop(0, n // tile)
     def _(i):
-        here = pl.ds(pl.multiple_of(i * tile, tile), tile)
+        here = pl.ds(start_of(i, tile), tile)
         first = mxu(xh[here, :], both)
         value = first[:, :r] + first[:, r:] + mxu(xl[here, :], wh)
         out_ref[here, :] = value.astype(BF)
@@ -160,15 +160,19 @@
         error[...] += jnp.sum((gap * gap).reshape(tile // 8, 8, r), axis=0)
 
 
+def start_of(i, tile):
+    return i * tile if isinstance(i, int) else pl.multiple_of(i * tile, tile)
+
+
 def split_tile(i, tile, valid_rows, x, y, xh, xl, yh, yl):
-    here = pl.ds(pl.multiple_of(i * tile, tile), tile)
+    here = pl.ds(start_of(i, tile), tile)
     valid = i * tile + lax.broadcasted_iota(jnp.int32, (tile, 1), 0) < valid_rows
     xh[here, :], xl[here, :] = halves_of(jnp.where(valid, x[...], 0.0))
     yh[here, :], yl[here, :] = halves_of(y[here, :])
 
 
 def upper_products(i, tile, xh, xl, yh, yl, upper, mirror, turned):
-    here = pl.ds(pl.multiple_of(i * tile, tile), tile)
+    here = pl.ds(start_of(i, tile), tile)
     half = xh.shape[1] // 2
     left, right = xh[here, :half], xh[here, half:]
     low = xl[here, :]
@@ -179,7 +183,7 @@
 
 
 def lower_products(i, tile, xh, xl, yh, yl, lower):
-    here = pl.ds(pl.multiple_of(i * tile, tile), tile)
+    here = pl.ds(start_of(i, tile), tile)
     half = xh.shape[1] // 2
     right = xh[here, half:]
     lower[...] += mxu(right, jnp.concatenate([yh[here, :], yl[here, :], xl[here, half:], right], axis=1), (0, 0))
@@ -274,9 +278,9 @@
     for peer in neighbours:
         pl.semaphore_signal(barrier, inc=1, device_id=peer, device_id_type=MESH)
     def load(i):
-        here = pl.ds(pl.multiple_of(i * tile, tile), tile)
+        here = pl.ds(start_of(i, tile), tile)
         return (
-            pltpu.make_async_copy(x_hbm.at[here], xf.at[lax.rem(i, slots)], loads.at[2 * i]),
+            pltpu.make_async_copy(x_hbm.at[here], xf.at[i % slots], loads.at[2 * i]),
             pltpu.make_async_copy(y_hbm.at[here], yf.at[here], loads.at[2 * i + 1]),
         )
 
@@ -393,17 +397,14 @@
     def split(i):
         for copy in load(i):
             copy.wait()
-        split_tile(i, tile, valid_rows, xf.at[lax.rem(i, slots)], yf, xh, xl, yh, yl)
+        split_tile(i, tile, valid_rows, xf.at[i % slots], yf, xh, xl, yh, yl)
 
     split(0)
 
-    @pl.loop(1, tiles)
-    def _(i):
-        @pl.when(i + slots - 1 < tiles)
-        def _():
+    for i in range(1, tiles):
+        if i + slots - 1 < tiles:
             for copy in load(i + slots - 1):
                 copy.start()
-
         upper_products(i - 1, tile, xh, xl, yh, yl, upper, mirror, turned)
         split(i)
 

time: 68.9 us -> 65.7 us (0.954)
  Pallas kernels: 63.8 us -> 60.6 us
    pallas_call x1, Pallas kernels: 63.8 us -> 60.6 us  [backtest(): pl.pallas_call(functools.partial(backtest_kernel, chunks, tile), in_specs...]
where the time goes in v5:
time: 65.7 us; the launch traced here: 65.6 us
  Pallas kernels  60.6 us (92%)
  local copies, waits for them, and re-layouts  2.62 us (4%)
  between operations  2.41 us (4%)
    pallas_call x1, Pallas kernels, backtest(): pl.pallas_call(functools.partial(backtest_kernel, chunks, tile), in_specs...  60.6 us
    unnamed x5, local copies, waits for them, and re-layouts  2.62 us

profile of v5, /device:TPU:65, one launch (start us, length us, event | category | flops | bytes accessed | tf_op | source)
XLA Modules:
  0.0 65.6 jit_solution(5093974183662100631)
XLA Ops:
  0.6 0.0 copy-start
  0.6 0.6 copy-done
  1.3 0.0 copy-start.1
  1.3 0.7 copy-done.1
  1.9 60.6 %backtest.1 = (bf16[8192,128]{1,0:T(8,128)(2,1)S(1)}, f32[1]{0:T(128)}) custom-call(s32[16]{0:T(128)S(1)} %copy-done, s32[16]{0:T(128)S(1)} %copy-done.1, f32[8192,512]{1,0:T(8,128)} %x_hbm.1, f32[8192,128]{1,0:T(8,128)} %y_hbm.1), custom_call_target="tpu_custom_call" | custom-call | tf_op jit(solution)/shard_map/backtest/pallas_call | solution.py:493
  62.5 1.3 %copy.8 = bf16[8192,128]{1,0:T(8,128)(2,1)} copy(bf16[8192,128]{1,0:T(8,128)(2,1)S(1)} %get-tuple-element.4) | data formatting | bytes 4194304
Async XLA Ops:
  0.6 0.7 %copy-start = (s32[16]{0:T(128)S(1)}, s32[16]{0:T(128)}, u32[]{:S(2)}) copy-start(s32[16]{0:T(128)} %counts_ref.1) | copy-start | bytes 196
  1.3 0.7 copy-start.1

commit v6 on v5

--- a/solution.py
+++ b/solution.py
@@ -149,8 +149,7 @@
     both = jnp.concatenate([wh, wl], axis=1)
     error[...] = jnp.zeros_like(error)
 
-    @pl.loop(0, n // tile)
-    def _(i):
+    for i in range(n // tile):
         here = pl.ds(start_of(i, tile), tile)
         first = mxu(xh[here, :], both)
         value = first[:, :r] + first[:, r:] + mxu(xl[here, :], wh)
@@ -414,14 +413,12 @@
     stage(0, 0)
     early = 2
 
-    @pl.loop(0, early)
-    def _(i):
+    for i in range(0, early):
         lower_products(i, tile, xh, xl, yh, yl, lower)
 
     stage(1, 0)
 
-    @pl.loop(early, tiles)
-    def _(i):
+    for i in range(early, tiles):
         lower_products(i, tile, xh, xl, yh, yl, lower)
 
     pack_lower(part_ref, lower, turned, f, targets)

time: 65.7 us -> 65.7 us (level)
  no operation moved by 1% of the time
where the time goes in v6:
time: 65.7 us; the launch traced here: 65.6 us
  Pallas kernels  60.6 us (92%)
  local copies, waits for them, and re-layouts  2.62 us (4%)
  between operations  2.41 us (4%)
    pallas_call x1, Pallas kernels, backtest(): pl.pallas_call(functools.partial(backtest_kernel, chunks, tile), in_specs...  60.6 us
    unnamed x5, local copies, waits for them, and re-layouts  2.62 us

profile of v6, /device:TPU:65, one launch (start us, length us, event | category | flops | bytes accessed | tf_op | source)
XLA Modules:
  0.0 65.6 jit_solution(4565926741189226885)
XLA Ops:
  0.6 0.0 copy-start
  0.6 0.6 copy-done
  1.3 0.0 copy-start.1
  1.3 0.7 copy-done.1
  1.9 60.6 %backtest.1 = (bf16[8192,128]{1,0:T(8,128)(2,1)S(1)}, f32[1]{0:T(128)}) custom-call(s32[16]{0:T(128)S(1)} %copy-done, s32[16]{0:T(128)S(1)} %copy-done.1, f32[8192,512]{1,0:T(8,128)} %x_hbm.1, f32[8192,128]{1,0:T(8,128)} %y_hbm.1), custom_call_target="tpu_custom_call" | custom-call | tf_op jit(solution)/shard_map/backtest/pallas_call | solution.py:490
  62.5 1.3 %copy.8 = bf16[8192,128]{1,0:T(8,128)(2,1)} copy(bf16[8192,128]{1,0:T(8,128)(2,1)S(1)} %get-tuple-element.4) | data formatting | bytes 4194304
Async XLA Ops:
  0.6 0.7 %copy-start = (s32[16]{0:T(128)S(1)}, s32[16]{0:T(128)}, u32[]{:S(2)}) copy-start(s32[16]{0:T(128)} %counts_ref.1) | copy-start | bytes 196
  1.3 0.7 copy-start.1
